TPU v7x, 32 devices: a whole 2x2x4 slice. The times are simulated.
32 devices in a mesh: outer: 8 (over z, core), inner: 4 (over y, x).
Axes of the slice: x: 2, y: 2, z: 4, core: 2. Of those that a mesh axis runs over, the one named last changes fastest.
Arguments:
- tokens: bfloat16 [4096, 12288], P(('outer', 'inner')), may hold values from -16 to 16
- cotangent: bfloat16 [4096, 128], P(('outer', 'inner')), may hold values from -8 to 8
- secondary: bfloat16 [12288, 128], P('inner'), may hold values from -0.0546875 to 0.0546875
- master: float32 [12288, 128], P(('inner', 'outer')), may hold values from -6 to 6
- m_code: bfloat16 [12288, 128], P(('inner', 'outer')), may hold values from -1 to 1
- v_code: bfloat16 [12288, 128], P(('inner', 'outer')), may hold values from 0.049804688 to 1
- m_scale: float32 [3072], P(('inner', 'outer')), may hold values from 0.02 to 0.2
- v_scale: float32 [3072], P(('inner', 'outer')), may hold values from 0.001 to 0.02
Outputs:
- projected: bfloat16 [4096, 128], P(('outer', 'inner'))
- master_new: float32 [12288, 128], P(('inner', 'outer'))
- m_code_new: bfloat16 [12288, 128], P(('inner', 'outer'))
- v_code_new: bfloat16 [12288, 128], P(('inner', 'outer'))
- m_scale_new: float32 [3072], P(('inner', 'outer'))
- v_scale_new: float32 [3072], P(('inner', 'outer'))
- secondary_new: bfloat16 [12288, 128], P('inner')
All inputs are finite; a program needn't handle non-finite values. Where the computation divides by a largest or mean magnitude, that divisor is 1e-20 or more.
Results may differ from a plain program's by a relative error of at most 0.009.
Values may be sent and summed in bfloat16 or wider, within the bound.
A program may use at most 64 MiB of HBM per device.

v0:
```python
import math

import jax
import jax.numpy as jnp
from jax import lax
from jax.sharding import PartitionSpec as P


def adam_update(gradient, factor, master, m_code, v_code, m_scale, v_scale):
    blocks = m_scale.shape[0]
    height = master.shape[0] // blocks
    shaped = (blocks, height, master.shape[1])
    m_old = (m_code.astype(jnp.float32).reshape(shaped) * m_scale[:, None, None]).reshape(
        master.shape
    )
    v_old = (v_code.astype(jnp.float32).reshape(shaped) * v_scale[:, None, None]).reshape(
        master.shape
    )
    scaled = factor * gradient
    moment = 0.9 * m_old + 0.1 * scaled
    second = 0.95 * v_old + 0.05 * scaled * scaled
    master_new = master - 0.01 * (moment / (jnp.sqrt(second) + 1e-08) + 0.1 * master)
    moment_blocks = moment.reshape(blocks, -1)
    second_blocks = second.reshape(blocks, -1)
    m_scale_new = jnp.max(jnp.abs(moment_blocks), axis=1) + 1e-06
    v_scale_new = jnp.max(second_blocks, axis=1) + 1e-06
    m_code_new = (moment_blocks / m_scale_new[:, None]).reshape(master.shape).astype(jnp.bfloat16)
    v_code_new = (second_blocks / v_scale_new[:, None]).reshape(master.shape).astype(jnp.bfloat16)
    return (master_new, m_code_new, v_code_new, m_scale_new, v_scale_new)


def rounded_term(columns, cotangent):
    part = lax.dot_general(
        columns, cotangent, (((0,), (0,)), ((), ())), preferred_element_type=jnp.float32
    )
    part = lax.optimization_barrier(part.astype(jnp.bfloat16))
    return part.astype(jnp.float32)


def body(tokens, cotangent, secondary, master, m_code, v_code, m_scale, v_scale):
    tok_rows = tokens.shape[0]
    width = tokens.shape[1]
    n_outer = lax.axis_size("outer")
    n_inner = lax.axis_size("inner")
    columns = tokens
    projected = jnp.dot(
        columns,
        lax.all_gather(secondary, "inner", axis=0, tiled=True),
        preferred_element_type=jnp.float32,
    ).astype(jnp.bfloat16)
    reordered = (
        tokens.reshape(tok_rows, n_inner, n_outer, -1)
        .transpose(0, 2, 1, 3)
        .reshape(tok_rows, width)
    )
    columns = reordered
    gradient = lax.psum_scatter(
        rounded_term(columns, cotangent), ("outer", "inner"), scatter_dimension=0, tiled=True
    )
    total = lax.psum(jnp.sum(gradient * gradient), ("outer", "inner"))
    limit = 0.25 * math.sqrt(width * secondary.shape[1])
    factor = limit / jnp.maximum(jnp.sqrt(total), limit)
    master_new, m_code_new, v_code_new, m_scale_new, v_scale_new = adam_update(
        gradient, factor, master, m_code, v_code, m_scale, v_scale
    )
    secondary_new = lax.all_gather(master_new.astype(jnp.bfloat16), "outer", axis=0, tiled=True)
    return (projected, master_new, m_code_new, v_code_new, m_scale_new, v_scale_new, secondary_new)


def solution(mesh):
    in_specs = (
        P(("outer", "inner"), None),
        P(("outer", "inner"), None),
        P("inner", None),
        P(("inner", "outer"), None),
        P(("inner", "outer"), None),
        P(("inner", "outer"), None),
        P(("inner", "outer")),
        P(("inner", "outer")),
    )
    out_specs = (
        P(("outer", "inner"), None),
        P(("inner", "outer"), None),
        P(("inner", "outer"), None),
        P(("inner", "outer"), None),
        P(("inner", "outer")),
        P(("inner", "outer")),
        P("inner", None),
    )
    return jax.shard_map(body, mesh=mesh, in_specs=in_specs, out_specs=out_specs, check_vma=False)
```

profile of v0, /device:TPU:0, one launch (start us, length us, event | category | flops | bytes accessed | tf_op | source)
XLA Modules:
  0.0 207.9 jit_solution(14521558974137962371)
XLA Ops:
  8.0 0.0 copy-start
  8.0 0.0 reduce-scatter.2.cloned.1.call-start
  8.1 3.5 %copy.15 = bf16[128,12288]{0,1:T(8,128)(2,1)S(1)} copy(bf16[128,12288]{1,0:T(8,128)(2,1)} %param.8) | data formatting | bytes 6291456 | tf_op args[0]
  11.5 0.2 copy.16
  11.8 1.0 convolution_convert_fusion
  12.7 2.9 %convert_element_type.27 = f32[12288,128]{1,0:T(8,128)} convert(bf16[12288,128]{1,0:T(8,128)(2,1)S(1)} %convolution_convert_fusion) | non-fusion elementwise | flops 1572864 | bytes 9437184 | tf_op jit(solution)/shard_map/convert_element_type | solution.py:37
  15.6 0.0 reduce-scatter.2.cloned.1.call-update
  15.7 0.0 all-gather.2.cloned.1.call-start
  15.7 0.5 all-gather.2.cloned.1.call-update
  16.2 0.0 copy-done.6
  16.3 0.1 mul.68
  16.4 0.1 mul.69
  16.5 0.1 mul.78
  16.6 0.1 mul.79
  16.7 116.2 %reduce-scatter.2.cloned.1.call-done = f32[384,128]{1,0:T(8,128)} async-done(((f32[12288,128]{1,0:T(8,128)}), f32[384,128]{1,0:T(8,128)}) %reduce-scatter.2.cloned.1.call-update) | async-done | bytes 196624 | tf_op jit(solution)/shard_map/reduce_scatter | solution.py:57
  132.9 1.6 multiply_reduce_fusion
  134.5 3.5 %convolution_convert_fusion.1 = bf16[128,128]{1,0:T(8,128)(2,1)} fusion(bf16[128,12288]{1,0:T(8,128)(2,1)S(1)} %copy-done.1, bf16[12288,128]{1,0:T(8,128)(2,1)} %all-gather.2.cloned.1.call-done), kind=kOutput, calls=%fused_computation.1 | convolution fusion | flops 402669568 | bytes 6324224 | tf_op jit(solution)/shard_map/dot_general | solution.py:46
  138.0 40.4 %psum.7 = f32[]{:T(128)} all-reduce(f32[]{:T(128)} %multiply_reduce_fusion), channel_id=1, replica_groups=mesh['outer'=8,'inner'=4] {'outer','inner'}, use_global_device_ids=true, to_apply=%region_2.0 | all-reduce | flops 1 | bytes 8 | tf_op jit(solution)/shard_map/psum | solution.py:60
  179.2 1.9 fusion.1
  181.1 0.1 reduce_max.24
  181.2 0.1 reduce_max.36
  181.3 0.1 reduce_max.25
  181.4 0.1 reduce_max.37
  181.6 0.0 copy-start.4
  181.6 0.0 copy-start.5
  181.6 0.1 div.34
  181.6 0.1 div.35
  181.8 0.1 div.38
  181.8 0.1 div.39
  182.0 15.7 %all_gather.7 = bf16[3072,128]{1,0:T(8,128)(2,1)S(1)} all-gather(bf16[384,128]{1,0:T(8,128)(2,1)S(1)} %get-tuple-element.11), channel_id=1, replica_groups=mesh['outer'=8,'inner'=4] {'outer'}, dimensions={0}, use_global_device_ids=true | all-gather | bytes 884736 | tf_op jit(solution)/shard_map/all_gather | solution.py:66
  197.7 1.8 divide_convert_fusion
  199.5 0.9 copy.18
  (14 shorter events, 0.0 us)
Async XLA Ops:
  8.0 3.8 %copy-start = (bf16[128,128]{1,0:T(8,128)(2,1)S(1)}, bf16[128,128]{1,0:T(8,128)(2,1)}, u32[]{:S(2)}) copy-start(bf16[128,128]{1,0:T(8,128)(2,1)} %param.9) | copy-start | bytes 98308
  8.0 124.9 %reduce-scatter.2.cloned.1.call-start = ((), (), s32[]{:S(2)}) async-start(), calls=%async_computation.2 | async-start | bytes 6488064 | tf_op jit(solution)/shard_map/reduce_scatter | solution.py:57
  15.6 0.7 copy-start.6
  15.6 0.8 copy-start.7
  15.6 118.8 %copy-start.1 = (bf16[128,12288]{1,0:T(8,128)(2,1)S(1)}, bf16[128,12288]{1,0:T(8,128)(2,1)}, u32[]{:S(2)}) copy-start(bf16[128,12288]{1,0:T(8,128)(2,1)} %param.8) | copy-start | bytes 9437188
  15.7 118.8 %all-gather.2.cloned.1.call-start = ((), (), s32[]{:S(2)}) async-start(), calls=%async_computation.1 | async-start | bytes 3932160 | tf_op jit(solution)/shard_map/all_gather | solution.py:48
  134.5 44.7 %copy-start.2 = (f32[384,128]{1,0:T(8,128)S(1)}, f32[384,128]{1,0:T(8,128)}, u32[]{:S(2)}) copy-start(f32[384,128]{1,0:T(8,128)} %reduce-scatter.2.cloned.1.call-done) | copy-start | bytes 589828
  134.5 44.7 %copy-start.3 = (bf16[384,128]{1,0:T(8,128)(2,1)S(1)}, bf16[384,128]{1,0:T(8,128)(2,1)}, u32[]{:S(2)}) copy-start(bf16[384,128]{1,0:T(8,128)(2,1)} %param.13) | copy-start | bytes 294916
  181.6 18.9 %copy-start.4 = (f32[96]{0:T(128)}, f32[96]{0:T(128)S(1)}, u32[]{:S(2)}) copy-start(f32[96]{0:T(128)S(1)} %get-tuple-element.29) | copy-start | bytes 1156
  181.6 18.9 %copy-start.5 = (f32[96]{0:T(128)}, f32[96]{0:T(128)S(1)}, u32[]{:S(2)}) copy-start(f32[96]{0:T(128)S(1)} %get-tuple-element.28) | copy-start | bytes 1156
Sparse Core Ops, SparseCore 0:
  15.8 117.0 reduce-scatter.1
Sparse Core Ops, SparseCore 1:
  18.0 46.5 all-gather.1
where the time goes:
time: 208 us
  waiting for transfers between devices  117 us (56%)
  blocking collectives  56.2 us (27%)
  between operations  16.3 us (8%)
  other arithmetic  8.44 us (4%)
  local copies, waits for them, and re-layouts  5.61 us (3%)
  matrix products  4.48 us (2%)
    reduce_scatter x1, waiting for transfers between devices, body(): lax.psum_scatter(rounded_term(columns, cotangent), ('outer', 'inner'), sc...  116 us
    psum x1, blocking collectives, body(): total = lax.psum(jnp.sum(gradient * gradient), ('outer', 'inner'))  40.4 us
    all_gather x1, blocking collectives, body(): lax.all_gather(master_new.astype(jnp.bfloat16), 'outer', axis=0, tiled=True)  15.7 us
    unnamed x18, local copies, waits for them, and re-layouts  4.45 us
  transfers between devices with their start and end apart: 2, of which 1 were waited for; matrix products, arithmetic and copies ran while one was open for 1% of the time, Pallas kernels for 0%

commit v1 on v0

--- a/solution.py
+++ b/solution.py
@@ -1,9 +1,16 @@
+import functools
 import math
 
 import jax
 import jax.numpy as jnp
 from jax import lax
+from jax.experimental import pallas as pl
+from jax.experimental.pallas import tpu as pltpu
 from jax.sharding import PartitionSpec as P
+
+MESH = pl.DeviceIdType.MESH
+PIECE = 128
+STEPS = (2, 1, 3, 0)
 
 
 def adam_update(gradient, factor, master, m_code, v_code, m_scale, v_scale):
@@ -67,6 +74,284 @@
     return (projected, master_new, m_code_new, v_code_new, m_scale_new, v_scale_new, secondary_new)
 
 
+def step_kernel(
+    limit,
+    tok, cot, sec, master, m_code, v_code, m_scale, v_scale,
+    projected, master_new, m_code_new, v_code_new, m_scale_new, v_scale_new, sec_new,
+    send_a, recv_a, send_1, recv_1, sum_2, send_2, recv_2, sum_3, send_3, recv_3,
+    weights, sq_1, sq_2, sq_send, moments, seconds,
+    sem_a, sem_1, sem_2, sem_3, sem_w, sem_f, sem_q1, sem_q2, sem_g, sem_h,
+):
+    f32, bf16 = jnp.float32, jnp.bfloat16
+    o, i = lax.axis_index("outer"), lax.axis_index("inner")
+    n_z = 4
+    core, z = o % 2, o // 2
+    x, y = i % 2, i // 2
+    to_x, to_y = i + 1 - 2 * x, i + 2 - 4 * y
+    first = to_x * (1 - core) + to_y * core
+    second = to_x * core + to_y * (1 - core)
+    across = 3 - i
+    mate = o + 1 - 2 * core
+    rows = master.shape[0]
+    half = sec.shape[0] // 2
+    span = sec.shape[0]
+
+    barrier = pltpu.get_barrier_semaphore()
+    near = [(o, first), (o, second), (o, across)]
+    far = [((o + d) % 8, i) for d in range(1, 8)]
+    for peer in near + far:
+        pl.semaphore_signal(barrier, inc=1, device_id=peer, device_id_type=MESH)
+
+    started = []
+
+    def send(src, dst, sems, index, peer):
+        copy = pltpu.make_async_remote_copy(
+            src_ref=src, dst_ref=dst,
+            send_sem=sems.at[0, index], recv_sem=sems.at[1, index],
+            device_id=peer, device_id_type=MESH,
+        )
+        copy.start()
+        started.append(copy)
+        return copy
+
+    def arrived(dst, sems, index):
+        pltpu.make_async_remote_copy(
+            src_ref=dst, dst_ref=dst,
+            send_sem=sems.at[0, index], recv_sem=sems.at[1, index],
+            device_id=(mate, i), device_id_type=MESH,
+        ).wait_recv()
+
+    def partial(j, s, c):
+        block = j * 8 + ((z + STEPS[s]) % n_z) * 2 + c
+        columns = tok[:, pl.ds(pl.multiple_of(block * rows, 128), rows)]
+        return lax.dot_general(
+            columns, cot[...], (((0,), (0,)), ((), ())), preferred_element_type=f32
+        )
+
+    for q, j in enumerate((across, second, first, i)):
+        for s in range(4):
+            send_a[q, s] = partial(j, s, 1 - core).astype(bf16)
+            if q == 0 and s == 0:
+                pl.semaphore_wait(barrier, 10)
+            send(send_a.at[q, s], recv_a.at[q, s], sem_a, q * 4 + s, (mate, i))
+
+    def chip_sum(q, j, s):
+        own = partial(j, s, core)
+        arrived(recv_a.at[q, s], sem_a, q * 4 + s)
+        return own + recv_a[q, s].astype(f32)
+
+    for q, j in enumerate((across, first)):
+        for s in range(4):
+            send_1[q, s] = chip_sum(q, j, s).astype(bf16)
+            send(send_1.at[q, s], recv_1.at[q, s], sem_1, q * 4 + s, (o, first))
+    for s in range(4):
+        sum_2[s] = chip_sum(2, second, s)
+    for s in range(4):
+        arrived(recv_1.at[0, s], sem_1, s)
+        send_2[s] = (sum_2[s] + recv_1[0, s].astype(f32)).astype(bf16)
+        send(send_2.at[s], recv_2.at[s], sem_2, s, (o, second))
+    for s in range(4):
+        sum_3[s] = chip_sum(3, i, s)
+
+    own_half = sec.at[pl.ds(pl.multiple_of(core * half, 128), half)]
+    for index, peer in enumerate((first, second)):
+        send(own_half, weights.at[i, core], sem_w, index, (o, peer))
+
+    gradient = None
+    for s in range(4):
+        arrived(recv_1.at[1, s], sem_1, 4 + s)
+        arrived(recv_2.at[s], sem_2, s)
+        total = sum_3[s] + recv_1[1, s].astype(f32) + recv_2[s].astype(f32)
+        if STEPS[s]:
+            d = STEPS[s]
+            send_3[d - 1] = total.astype(bf16)
+            peer = ((z + d) % n_z) * 2 + core
+            send(send_3.at[d - 1], recv_3.at[d - 1], sem_3, d - 1, (peer, i))
+        else:
+            sum_3[0] = total
+
+    own_columns = tok[:, pl.ds(pl.multiple_of(i * span, 128), span)]
+    out = jnp.dot(own_columns, sec[...], preferred_element_type=f32)
+
+    for d in (1, 3, 2):
+        arrived(recv_3.at[d - 1], sem_3, d - 1)
+    gradient = sum_3[0]
+    for d in range(1, 4):
+        gradient = gradient + recv_3[d - 1].astype(f32)
+    sum_3[0] = gradient
+
+    squares = jnp.sum((gradient * gradient).reshape(rows // 8, 8, 128), axis=0)
+    sq_send[0] = squares
+    for index, peer in enumerate((first, second, across)):
+        send(sq_send.at[0], sq_1.at[index], sem_q1, index, (o, peer))
+    for index in range(3):
+        arrived(sq_1.at[index], sem_q1, index)
+        squares = squares + sq_1[index]
+    sq_send[1] = squares
+    for d in range(1, 8):
+        send(sq_send.at[1], sq_2.at[d - 1], sem_q2, d - 1, ((o + d) % 8, i))
+
+    height = rows // m_scale.shape[1]
+
+    def block_mask(p):
+        shape = (PIECE, m_scale.shape[1])
+        row = lax.broadcasted_iota(jnp.int32, shape, 0) + p * PIECE
+        return row // height == lax.broadcasted_iota(jnp.int32, shape, 1)
+
+    def expand(p, scales):
+        return jnp.sum(jnp.where(block_mask(p), scales, 0.0), axis=1, keepdims=True)
+
+    pieces = rows // PIECE
+    for p in range(pieces):
+        part = pl.ds(p * PIECE, PIECE)
+        moments[part, :] = 0.9 * (m_code[part, :].astype(f32) * expand(p, m_scale[...]))
+        seconds[part, :] = 0.95 * (v_code[part, :].astype(f32) * expand(p, v_scale[...]))
+
+    for d in range(1, 8):
+        arrived(sq_2.at[d - 1], sem_q2, d - 1)
+        squares = squares + sq_2[d - 1]
+    square_sum = jnp.sum(jnp.sum(squares, axis=0, keepdims=True), axis=1, keepdims=True)
+    factor = limit / jnp.maximum(jnp.sqrt(square_sum), limit)
+
+    for p in range(pieces):
+        part = pl.ds(p * PIECE, PIECE)
+        scaled = factor * sum_3[0, part, :]
+        moment = moments[part, :] + 0.1 * scaled
+        second_new = seconds[part, :] + 0.05 * scaled * scaled
+        old = master[part, :]
+        new = old - 0.01 * (moment / (jnp.sqrt(second_new) + 1e-08) + 0.1 * old)
+        moments[part, :] = moment
+        seconds[part, :] = second_new
+        master_new[part, :] = new
+        sec_new[pl.ds(pl.multiple_of(o * rows + p * PIECE, 128), PIECE), :] = new.astype(bf16)
+
+    def new_rows(owner):
+        return sec_new.at[pl.ds(pl.multiple_of(owner * rows, 128), rows)]
+
+    for d in (2, 1, 3):
+        send(new_rows(o), new_rows(o), sem_g, d - 1, (((z + d) % n_z) * 2 + core, i))
+    send(new_rows(o), new_rows(o), sem_h, 0, (mate, i))
+
+    arrived(weights.at[first, core], sem_w, 0)
+    send(weights.at[first, core], weights.at[first, core], sem_w, 2, (o, second))
+    send(weights.at[first, core], weights.at[first, core], sem_f, 0, (mate, i))
+    arrived(weights.at[second, core], sem_w, 1)
+    send(weights.at[second, core], weights.at[second, core], sem_f, 1, (mate, i))
+
+    m_row = jnp.zeros(m_scale.shape, f32)
+    v_row = jnp.zeros(v_scale.shape, f32)
+    for p in range(pieces):
+        part = pl.ds(p * PIECE, PIECE)
+        mask = block_mask(p)
+        for values, codes, is_m in ((moments, m_code_new, True), (seconds, v_code_new, False)):
+            value = values[part, :]
+            tops = jnp.max(jnp.abs(value), axis=1, keepdims=True)
+            top = jnp.max(jnp.where(mask, tops, 0.0), axis=0, keepdims=True)
+            scale = top + 1e-06
+            codes[part, :] = (value / expand(p, scale)).astype(bf16)
+            if is_m:
+                m_row = jnp.maximum(m_row, top)
+            else:
+                v_row = jnp.maximum(v_row, top)
+    m_scale_new[...] = m_row + 1e-06
+    v_scale_new[...] = v_row + 1e-06
+
+    def product(j, h):
+        start = pl.multiple_of(j * span + h * half, 128)
+        return jnp.dot(tok[:, pl.ds(start, half)], weights[j, h], preferred_element_type=f32)
+
+    out = out + product(first, core)
+    out = out + product(second, core)
+
+    def gathered(d):
+        owner = ((z + n_z - d) % n_z) * 2 + core
+        arrived(new_rows(owner), sem_g, d - 1)
+        send(new_rows(owner), new_rows(owner), sem_h, d, (mate, i))
+
+    gathered(1)
+    arrived(weights.at[across, core], sem_w, 2)
+    send(weights.at[across, core], weights.at[across, core], sem_f, 2, (mate, i))
+    out = out + product(across, core)
+    for index, j in enumerate((second, first)):
+        arrived(weights.at[j, 1 - core], sem_f, index)
+        out = out + product(j, 1 - core)
+    gathered(3)
+    arrived(weights.at[across, 1 - core], sem_f, 2)
+    out = out + product(across, 1 - core)
+    projected[...] = out.astype(bf16)
+    gathered(2)
+    for d in range(4):
+        owner = ((z + n_z - d) % n_z) * 2 + 1 - core
+        arrived(new_rows(owner), sem_h, d)
+    for copy in started:
+        copy.wait_send()
+
+
+def fused_body(tokens, cotangent, secondary, master, m_code, v_code, m_scale, v_scale):
+    f32, bf16 = jnp.float32, jnp.bfloat16
+    rows, head = master.shape
+    blocks = m_scale.shape[0]
+    chunk = (rows, head)
+    limit = 0.25 * math.sqrt(tokens.shape[1] * secondary.shape[1])
+    vmem, dma = pltpu.VMEM, pltpu.SemaphoreType.DMA
+    shapes = (
+        ((tokens.shape[0], head), bf16),
+        (chunk, f32),
+        (chunk, bf16),
+        (chunk, bf16),
+        ((1, blocks), f32),
+        ((1, blocks), f32),
+        (secondary.shape, bf16),
+    )
+    work = 4 * tokens.shape[0] * tokens.shape[1] * head
+    outs = pl.pallas_call(
+        functools.partial(step_kernel, limit),
+        out_shape=[jax.ShapeDtypeStruct(shape, dtype) for shape, dtype in shapes],
+        in_specs=[pl.BlockSpec(memory_space=vmem)] * 8,
+        out_specs=[pl.BlockSpec(memory_space=vmem)] * 7,
+        scratch_shapes=[
+            vmem((4, 4) + chunk, bf16),
+            vmem((4, 4) + chunk, bf16),
+            vmem((2, 4) + chunk, bf16),
+            vmem((2, 4) + chunk, bf16),
+            vmem((4,) + chunk, f32),
+            vmem((4,) + chunk, bf16),
+            vmem((4,) + chunk, bf16),
+            vmem((4,) + chunk, f32),
+            vmem((3,) + chunk, bf16),
+            vmem((3,) + chunk, bf16),
+            vmem((4, 2, secondary.shape[0] // 2, head), bf16),
+            vmem((3, 8, head), f32),
+            vmem((7, 8, head), f32),
+            vmem((2, 8, head), f32),
+            vmem(chunk, f32),
+            vmem(chunk, f32),
+            dma((2, 16)),
+            dma((2, 8)),
+            dma((2, 4)),
+            dma((2, 3)),
+            dma((2, 3)),
+            dma((2, 3)),
+            dma((2, 3)),
+            dma((2, 7)),
+            dma((2, 3)),
+            dma((2, 4)),
+        ],
+        compiler_params=pltpu.CompilerParams(
+            collective_id=0, has_side_effects=True, vmem_limit_bytes=48 * 1024 * 1024
+        ),
+        cost_estimate=pl.CostEstimate(flops=work, bytes_accessed=8 << 20, transcendentals=0),
+    )(
+        tokens, cotangent, secondary, master, m_code, v_code,
+        m_scale.reshape(1, blocks), v_scale.reshape(1, blocks),
+    )
+    return (*outs[:4], outs[4].reshape(blocks), outs[5].reshape(blocks), outs[6])
+
+
+def fits(mesh):
+    return mesh.shape["outer"] == 8 and mesh.shape["inner"] == 4
+
+
 def solution(mesh):
     in_specs = (
         P(("outer", "inner"), None),
@@ -87,4 +372,7 @@
         P(("inner", "outer")),
         P("inner", None),
     )
-    return jax.shard_map(body, mesh=mesh, in_specs=in_specs, out_specs=out_specs, check_vma=False)
+    program = fused_body if fits(mesh) else body
+    return jax.shard_map(
+        program, mesh=mesh, in_specs=in_specs, out_specs=out_specs, check_vma=False
+    )

time: 208 us -> 62.7 us (0.30)
  waiting for transfers between devices: 117 us -> 0 us
  blocking collectives: 56.2 us -> 0 us
  Pallas kernels: 0 us -> 49.4 us
  between operations: 16.3 us -> 0.66 us
  other arithmetic: 8.44 us -> 0 us
  local copies, waits for them, and re-layouts: 5.61 us -> 12.3 us
  matrix products: 4.48 us -> 0 us
    reduce_scatter x1 -> x0, waiting for transfers between devices: 116 us -> none  [body(): lax.psum_scatter(rounded_term(columns, cotangent), ('outer', 'inner'), sc...]
    pallas_call x0 -> x1, Pallas kernels: none -> 49.4 us  [fused_body(): pl.pallas_call(functools.partial(step_kernel, limit), out_shape=[jax.Shap...]
    psum x1 -> x0, blocking collectives: 40.4 us -> none  [body(): total = lax.psum(jnp.sum(gradient * gradient), ('outer', 'inner'))]
    all_gather x1 -> x0, blocking collectives: 15.7 us -> none  [body(): lax.all_gather(master_new.astype(jnp.bfloat16), 'outer', axis=0, tiled=True)]
    unnamed x18 -> x23, local copies, waits for them, and re-layouts: 4.45 us -> 12.3 us
    convert_element_type x2 -> x0, other arithmetic: 4.73 us -> none  [the longest x1 2.89 us: rounded_term(): return part.astype(jnp.float32)]
    dot_general x2 -> x0, matrix products: 4.48 us -> none  [the longest x1 3.52 us: body(): jnp.dot(columns, lax.all_gather(secondary, 'inner', axis=0, tiled=True),...]
    reduce_max x3 -> x0, other arithmetic: 2.13 us -> none  [the longest x2 2.02 us: adam_update(): v_scale_new = jnp.max(second_blocks, axis=1) + 1e-06]
  transfers between devices with their start and end apart: 2 -> 0, of which waited for: 1 -> 0; matrix products, arithmetic and copies ran while one was open for 1% -> 0% of each run, Pallas kernels for 0% -> 0%
where the time goes in v1:
time: 62.7 us; the launch traced here: 62.4 us
  Pallas kernels  49.4 us (79%)
  local copies, waits for them, and re-layouts  12.3 us (20%)
  between operations  0.66 us (1%)
    pallas_call x1, Pallas kernels, fused_body(): pl.pallas_call(functools.partial(step_kernel, limit), out_shape=[jax.Shap...  49.4 us
    unnamed x23, local copies, waits for them, and re-layouts  12.3 us

profile of v1, /device:TPU:0, one launch (start us, length us, event | category | flops | bytes accessed | tf_op | source)
XLA Modules:
  0.0 62.4 jit_solution(4108598649555655643)
XLA Ops:
  0.6 0.0 copy-start
  0.6 1.9 %copy-done = bf16[128,12288]{1,0:T(8,128)(2,1)S(1)} copy-done((bf16[128,12288]{1,0:T(8,128)(2,1)S(1)}, bf16[128,12288]{1,0:T(8,128)(2,1)}, u32[]{:S(2)}) %copy-start) | copy-done | bytes 3145752
  2.5 0.0 copy-start.1
  2.5 1.1 %copy-done.1 = bf16[3072,128]{1,0:T(8,128)(2,1)S(1)} copy-done((bf16[3072,128]{1,0:T(8,128)(2,1)S(1)}, bf16[3072,128]{1,0:T(8,128)(2,1)}, u32[]{:S(2)}) %copy-start.1) | copy-done | bytes 786456
  3.7 0.0 copy-start.2
  3.7 0.9 %copy-done.2 = f32[384,128]{1,0:T(8,128)S(1)} copy-done((f32[384,128]{1,0:T(8,128)S(1)}, f32[384,128]{1,0:T(8,128)}, u32[]{:S(2)}) %copy-start.2) | copy-done | bytes 196632
  4.6 0.0 copy-start.3
  4.6 0.9 %copy-done.3 = bf16[384,128]{1,0:T(8,128)(2,1)S(1)} copy-done((bf16[384,128]{1,0:T(8,128)(2,1)S(1)}, bf16[384,128]{1,0:T(8,128)(2,1)}, u32[]{:S(2)}) %copy-start.3) | copy-done | bytes 98328
  5.5 0.0 copy-start.4
  5.5 0.9 %copy-done.4 = bf16[384,128]{1,0:T(8,128)(2,1)S(1)} copy-done((bf16[384,128]{1,0:T(8,128)(2,1)S(1)}, bf16[384,128]{1,0:T(8,128)(2,1)}, u32[]{:S(2)}) %copy-start.4) | copy-done | bytes 98328
  6.4 0.0 copy-start.5
  6.4 0.8 %copy-done.5 = bf16[128,128]{1,0:T(8,128)(2,1)S(1)} copy-done((bf16[128,128]{1,0:T(8,128)(2,1)S(1)}, bf16[128,128]{1,0:T(8,128)(2,1)}, u32[]{:S(2)}) %copy-start.5) | copy-done | bytes 32792
  7.1 0.0 copy-start.6
  7.1 0.7 %copy-done.6 = f32[96]{0:T(128)S(1)} copy-done((f32[96]{0:T(128)S(1)}, f32[96]{0:T(128)}, u32[]{:S(2)}) %copy-start.6) | copy-done | bytes 408
  7.8 0.0 copy-start.7
  7.8 0.7 %copy-done.7 = f32[96]{0:T(128)S(1)} copy-done((f32[96]{0:T(128)S(1)}, f32[96]{0:T(128)}, u32[]{:S(2)}) %copy-start.7) | copy-done | bytes 408
  8.4 49.4 %shard_map.135 = (bf16[128,128]{1,0:T(8,128)(2,1)S(1)}, f32[384,128]{1,0:T(8,128)S(1)}, bf16[384,128]{1,0:T(8,128)(2,1)S(1)}, bf16[384,128]{1,0:T(8,128)(2,1)S(1...) custom-call(bf16[128,12288]{1,0:T(8,128)(2,1)S(1)} %copy-done, ...), custom_call_target="tpu_custom_call" | custom-call | flops 805306368 | bytes 8388608 | tf_op jit(solution)/shard_map/pallas_call | solution.py:307
  57.9 0.6 copy.22
  58.5 0.7 %copy.23 = f32[384,128]{1,0:T(8,128)} copy(f32[384,128]{1,0:T(8,128)S(1)} %get-tuple-element.29) | data formatting | bytes 393216
  59.2 0.6 %copy.24 = bf16[384,128]{1,0:T(8,128)(2,1)} copy(bf16[384,128]{1,0:T(8,128)(2,1)S(1)} %get-tuple-element.30) | data formatting | bytes 196608
  59.8 0.6 %copy.25 = bf16[384,128]{1,0:T(8,128)(2,1)} copy(bf16[384,128]{1,0:T(8,128)(2,1)S(1)} %get-tuple-element.31) | data formatting | bytes 196608
  60.5 0.5 copy.26
  61.0 0.5 copy.27
  61.5 0.9 %copy.28 = bf16[3072,128]{1,0:T(8,128)(2,1)} copy(bf16[3072,128]{1,0:T(8,128)(2,1)S(1)} %get-tuple-element.34) | data formatting | bytes 1572864
Async XLA Ops:
  0.6 1.9 %copy-start = (bf16[128,12288]{1,0:T(8,128)(2,1)S(1)}, bf16[128,12288]{1,0:T(8,128)(2,1)}, u32[]{:S(2)}) copy-start(bf16[128,12288]{1,0:T(8,128)(2,1)} %tok.1) | copy-start | bytes 9437188
  2.5 1.1 %copy-start.1 = (bf16[3072,128]{1,0:T(8,128)(2,1)S(1)}, bf16[3072,128]{1,0:T(8,128)(2,1)}, u32[]{:S(2)}) copy-start(bf16[3072,128]{1,0:T(8,128)(2,1)} %sec.1) | copy-start | bytes 2359300
  3.7 0.9 %copy-start.2 = (f32[384,128]{1,0:T(8,128)S(1)}, f32[384,128]{1,0:T(8,128)}, u32[]{:S(2)}) copy-start(f32[384,128]{1,0:T(8,128)} %master.1) | copy-start | bytes 589828
  4.6 0.9 %copy-start.3 = (bf16[384,128]{1,0:T(8,128)(2,1)S(1)}, bf16[384,128]{1,0:T(8,128)(2,1)}, u32[]{:S(2)}) copy-start(bf16[384,128]{1,0:T(8,128)(2,1)} %m_code.1) | copy-start | bytes 294916
  5.5 0.9 %copy-start.4 = (bf16[384,128]{1,0:T(8,128)(2,1)S(1)}, bf16[384,128]{1,0:T(8,128)(2,1)}, u32[]{:S(2)}) copy-start(bf16[384,128]{1,0:T(8,128)(2,1)} %v_code.1) | copy-start | bytes 294916
  6.4 0.8 %copy-start.5 = (bf16[128,128]{1,0:T(8,128)(2,1)S(1)}, bf16[128,128]{1,0:T(8,128)(2,1)}, u32[]{:S(2)}) copy-start(bf16[128,128]{1,0:T(8,128)(2,1)} %cot.1) | copy-start | bytes 98308
  7.1 0.7 %copy-start.6 = (f32[96]{0:T(128)S(1)}, f32[96]{0:T(128)}, u32[]{:S(2)}) copy-start(f32[96]{0:T(128)} %param.14) | copy-start | bytes 1156
  7.8 0.7 %copy-start.7 = (f32[96]{0:T(128)S(1)}, f32[96]{0:T(128)}, u32[]{:S(2)}) copy-start(f32[96]{0:T(128)} %param.15) | copy-start | bytes 1156

commit v2 on v1

--- a/solution.py
+++ b/solution.py
@@ -10,6 +10,7 @@
 
 MESH = pl.DeviceIdType.MESH
 PIECE = 128
+VMEM_BYTES = 60 * 1024 * 1024
 STEPS = (2, 1, 3, 0)
 
 
@@ -76,11 +77,13 @@
 
 def step_kernel(
     limit,
+    tok_in, cot_in, sec_in, master_in, m_code_in, v_code_in, m_scale_in, v_scale_in,
+    projected_out, master_out, m_code_out, v_code_out, m_scale_out, v_scale_out, sec_out,
+    projected, master_new, m_code_new, v_code_new, m_scale_new, v_scale_new, sec_new,
     tok, cot, sec, master, m_code, v_code, m_scale, v_scale,
-    projected, master_new, m_code_new, v_code_new, m_scale_new, v_scale_new, sec_new,
     send_a, recv_a, send_1, recv_1, sum_2, send_2, recv_2, sum_3, send_3, recv_3,
     weights, sq_1, sq_2, sq_send, moments, seconds,
-    sem_a, sem_1, sem_2, sem_3, sem_w, sem_f, sem_q1, sem_q2, sem_g, sem_h,
+    sem_in, sem_out, sem_a, sem_1, sem_2, sem_3, sem_w, sem_f, sem_q1, sem_q2, sem_g, sem_h,
 ):
     f32, bf16 = jnp.float32, jnp.bfloat16
     o, i = lax.axis_index("outer"), lax.axis_index("inner")
@@ -102,6 +105,29 @@
     for peer in near + far:
         pl.semaphore_signal(barrier, inc=1, device_id=peer, device_id_type=MESH)
 
+    loads = []
+
+    def load(src, dst):
+        loads.append(pltpu.make_async_copy(src, dst, sem_in.at[len(loads)]))
+        loads[-1].start()
+
+    stores = []
+
+    def store(src, dst):
+        stores.append(pltpu.make_async_copy(src, dst, sem_out.at[len(stores)]))
+        stores[-1].start()
+
+    load(cot_in, cot)
+    for j in (across, second, first, i):
+        columns = pl.ds(pl.multiple_of(j * span, 128), span)
+        load(tok_in.at[:, columns], tok.at[:, columns])
+    load(sec_in, sec)
+    load(master_in, master)
+    load(m_code_in, m_code)
+    load(v_code_in, v_code)
+    load(m_scale_in, m_scale)
+    load(v_scale_in, v_scale)
+
     started = []
 
     def send(src, dst, sems, index, peer):
@@ -128,36 +154,46 @@
             columns, cot[...], (((0,), (0,)), ((), ())), preferred_element_type=f32
         )
 
-    for q, j in enumerate((across, second, first, i)):
+    mate_groups = (across, second, first, i)
+    own_groups = (across, first, second, i)
+
+    def for_mate(q):
         for s in range(4):
-            send_a[q, s] = partial(j, s, 1 - core).astype(bf16)
+            send_a[q, s] = partial(mate_groups[q], s, 1 - core).astype(bf16)
             if q == 0 and s == 0:
                 pl.semaphore_wait(barrier, 10)
             send(send_a.at[q, s], recv_a.at[q, s], sem_a, q * 4 + s, (mate, i))
 
-    def chip_sum(q, j, s):
-        own = partial(j, s, core)
+    def chip_sum(q, s):
+        own = partial(own_groups[q], s, core)
         arrived(recv_a.at[q, s], sem_a, q * 4 + s)
         return own + recv_a[q, s].astype(f32)
 
-    for q, j in enumerate((across, first)):
+    def to_first(q):
         for s in range(4):
-            send_1[q, s] = chip_sum(q, j, s).astype(bf16)
+            send_1[q, s] = chip_sum(q, s).astype(bf16)
             send(send_1.at[q, s], recv_1.at[q, s], sem_1, q * 4 + s, (o, first))
+
+    loads[0].wait()
+    loads[1].wait()
+    for_mate(0)
+    loads[2].wait()
+    for_mate(1)
+    to_first(0)
+    loads[3].wait()
+    for_mate(2)
+    to_first(1)
+    loads[4].wait()
+    for_mate(3)
     for s in range(4):
-        sum_2[s] = chip_sum(2, second, s)
+        sum_2[s] = chip_sum(2, s)
+    for s in range(4):
+        sum_3[s] = chip_sum(3, s)
     for s in range(4):
         arrived(recv_1.at[0, s], sem_1, s)
         send_2[s] = (sum_2[s] + recv_1[0, s].astype(f32)).astype(bf16)
         send(send_2.at[s], recv_2.at[s], sem_2, s, (o, second))
-    for s in range(4):
-        sum_3[s] = chip_sum(3, i, s)
-
-    own_half = sec.at[pl.ds(pl.multiple_of(core * half, 128), half)]
-    for index, peer in enumerate((first, second)):
-        send(own_half, weights.at[i, core], sem_w, index, (o, peer))
-
-    gradient = None
+
     for s in range(4):
         arrived(recv_1.at[1, s], sem_1, 4 + s)
         arrived(recv_2.at[s], sem_2, s)
@@ -170,6 +206,11 @@
         else:
             sum_3[0] = total
 
+    loads[5].wait()
+    own_half = sec.at[pl.ds(pl.multiple_of(core * half, 128), half)]
+    for index, peer in enumerate((first, second)):
+        send(own_half, weights.at[i, core], sem_w, index, (o, peer))
+
     own_columns = tok[:, pl.ds(pl.multiple_of(i * span, 128), span)]
     out = jnp.dot(own_columns, sec[...], preferred_element_type=f32)
 
@@ -191,6 +232,8 @@
     for d in range(1, 8):
         send(sq_send.at[1], sq_2.at[d - 1], sem_q2, d - 1, ((o + d) % 8, i))
 
+    for copy in loads[6:]:
+        copy.wait()
     height = rows // m_scale.shape[1]
 
     def block_mask(p):
@@ -228,9 +271,14 @@
     def new_rows(owner):
         return sec_new.at[pl.ds(pl.multiple_of(owner * rows, 128), rows)]
 
+    def store_rows(owner):
+        store(new_rows(owner), sec_out.at[pl.ds(pl.multiple_of(owner * rows, 128), rows)])
+
     for d in (2, 1, 3):
         send(new_rows(o), new_rows(o), sem_g, d - 1, (((z + d) % n_z) * 2 + core, i))
     send(new_rows(o), new_rows(o), sem_h, 0, (mate, i))
+    store(master_new, master_out)
+    store_rows(o)
 
     arrived(weights.at[first, core], sem_w, 0)
     send(weights.at[first, core], weights.at[first, core], sem_w, 2, (o, second))
@@ -255,6 +303,10 @@
                 v_row = jnp.maximum(v_row, top)
     m_scale_new[...] = m_row + 1e-06
     v_scale_new[...] = v_row + 1e-06
+    store(m_code_new, m_code_out)
+    store(v_code_new, v_code_out)
+    store(m_scale_new, m_scale_out)
+    store(v_scale_new, v_scale_out)
 
     def product(j, h):
         start = pl.multiple_of(j * span + h * half, 128)
@@ -267,6 +319,7 @@
         owner = ((z + n_z - d) % n_z) * 2 + core
         arrived(new_rows(owner), sem_g, d - 1)
         send(new_rows(owner), new_rows(owner), sem_h, d, (mate, i))
+        store_rows(owner)
 
     gathered(1)
     arrived(weights.at[across, core], sem_w, 2)
@@ -279,12 +332,28 @@
     arrived(weights.at[across, 1 - core], sem_f, 2)
     out = out + product(across, 1 - core)
     projected[...] = out.astype(bf16)
+    store(projected, projected_out)
     gathered(2)
     for d in range(4):
         owner = ((z + n_z - d) % n_z) * 2 + 1 - core
         arrived(new_rows(owner), sem_h, d)
+        store_rows(owner)
+    for copy in stores:
+        copy.wait()
     for copy in started:
         copy.wait_send()
+
+
+def write_kernel(*refs):
+    count = len(refs) // 2
+    sems = refs[-1]
+    copies = [
+        pltpu.make_async_copy(refs[k], refs[count + k], sems.at[k]) for k in range(count)
+    ]
+    for copy in copies:
+        copy.start()
+    for copy in copies:
+        copy.wait()
 
 
 def fused_body(tokens, cotangent, secondary, master, m_code, v_code, m_scale, v_scale):
@@ -307,9 +376,18 @@
     outs = pl.pallas_call(
         functools.partial(step_kernel, limit),
         out_shape=[jax.ShapeDtypeStruct(shape, dtype) for shape, dtype in shapes],
-        in_specs=[pl.BlockSpec(memory_space=vmem)] * 8,
-        out_specs=[pl.BlockSpec(memory_space=vmem)] * 7,
+        in_specs=[pl.BlockSpec(memory_space=pltpu.HBM)] * 8,
+        out_specs=[pl.BlockSpec(memory_space=pltpu.HBM)] * 7,
         scratch_shapes=[
+            *(vmem(shape, dtype) for shape, dtype in shapes),
+            vmem(tokens.shape, bf16),
+            vmem(cotangent.shape, bf16),
+            vmem(secondary.shape, bf16),
+            vmem(chunk, f32),
+            vmem(chunk, bf16),
+            vmem(chunk, bf16),
+            vmem((1, blocks), f32),
+            vmem((1, blocks), f32),
             vmem((4, 4) + chunk, bf16),
             vmem((4, 4) + chunk, bf16),
             vmem((2, 4) + chunk, bf16),
@@ -326,6 +404,8 @@
             vmem((2, 8, head), f32),
             vmem(chunk, f32),
             vmem(chunk, f32),
+            dma((11,)),
+            dma((14,)),
             dma((2, 16)),
             dma((2, 8)),
             dma((2, 4)),
@@ -338,13 +418,21 @@
             dma((2, 4)),
         ],
         compiler_params=pltpu.CompilerParams(
-            collective_id=0, has_side_effects=True, vmem_limit_bytes=48 * 1024 * 1024
+            collective_id=0, has_side_effects=True, vmem_limit_bytes=VMEM_BYTES
         ),
         cost_estimate=pl.CostEstimate(flops=work, bytes_accessed=8 << 20, transcendentals=0),
     )(
         tokens, cotangent, secondary, master, m_code, v_code,
         m_scale.reshape(1, blocks), v_scale.reshape(1, blocks),
     )
+    outs = pl.pallas_call(
+        write_kernel,
+        out_shape=[jax.ShapeDtypeStruct(shape, dtype) for shape, dtype in shapes],
+        in_specs=[pl.BlockSpec(memory_space=pltpu.HBM)] * 7,
+        out_specs=[pl.BlockSpec(memory_space=pltpu.HBM)] * 7,
+        scratch_shapes=[dma((7,))],
+        compiler_params=pltpu.CompilerParams(vmem_limit_bytes=VMEM_BYTES),
+    )(*outs)
     return (*outs[:4], outs[4].reshape(blocks), outs[5].reshape(blocks), outs[6])
 
 

time: 62.7 us -> 88.9 us (1.42)
  Pallas kernels: 49.4 us -> 88.1 us
  local copies, waits for them, and re-layouts: 12.3 us -> 0 us
    pallas_call x0 -> x1, Pallas kernels: none -> 37.9 us  [fused_body(): pl.pallas_call(write_kernel, out_shape=[jax.ShapeDtypeStruct(shape, dtype...]
    unnamed x23 -> x0, local copies, waits for them, and re-layouts: 12.3 us -> none
where the time goes in v2:
time: 88.9 us; the launch traced here: 88.7 us
  Pallas kernels  88.1 us (99%)
    pallas_call x1, Pallas kernels, fused_body(): pl.pallas_call(functools.partial(step_kernel, limit), out_shape=[jax.Shap...  50.2 us
    pallas_call x1, Pallas kernels, fused_body(): pl.pallas_call(write_kernel, out_shape=[jax.ShapeDtypeStruct(shape, dtype...  37.9 us

profile of v2, /device:TPU:0, one launch (start us, length us, event | category | flops | bytes accessed | tf_op | source)
XLA Modules:
  0.0 88.7 jit_solution(4597279459425647378)
XLA Ops:
  0.6 50.2 %shard_map.135 = (bf16[128,128]{1,0:T(8,128)(2,1)}, f32[384,128]{1,0:T(8,128)}, bf16[384,128]{1,0:T(8,128)(2,1)}, bf16[384,128]{1,0:T(8,128)(2,1)}, f32[1,96]{1,...) custom-call(bf16[128,12288]{1,0:T(8,128)(2,1)} %tok_in.1, bf16[128,128]{1,0:T(8,128)(2,1)} %cot_in.1, ...), custom_call_target="tpu_custom_call" | custom-call | flops 805306368 | bytes 8388608 | tf_op jit(solution)/shard_map/pallas_call | solution.py:376
  50.8 37.9 %shard_map.136 = (bf16[128,128]{1,0:T(8,128)(2,1)}, f32[384,128]{1,0:T(8,128)}, bf16[384,128]{1,0:T(8,128)(2,1)}, bf16[384,128]{1,0:T(8,128)(2,1)}, f32[1,96]{1,...) custom-call(bf16[128,128]{1,0:T(8,128)(2,1)} %get-tuple-element.21.refs_0_, ...), custom_call_target="tpu_custom_call" | custom-call | tf_op jit(solution)/shard_map/pallas_call | solution.py:428

commit v3 on v2

--- a/solution.py
+++ b/solution.py
@@ -78,12 +78,11 @@
 def step_kernel(
     limit,
     tok_in, cot_in, sec_in, master_in, m_code_in, v_code_in, m_scale_in, v_scale_in,
-    projected_out, master_out, m_code_out, v_code_out, m_scale_out, v_scale_out, sec_out,
     projected, master_new, m_code_new, v_code_new, m_scale_new, v_scale_new, sec_new,
     tok, cot, sec, master, m_code, v_code, m_scale, v_scale,
     send_a, recv_a, send_1, recv_1, sum_2, send_2, recv_2, sum_3, send_3, recv_3,
     weights, sq_1, sq_2, sq_send, moments, seconds,
-    sem_in, sem_out, sem_a, sem_1, sem_2, sem_3, sem_w, sem_f, sem_q1, sem_q2, sem_g, sem_h,
+    sem_in, sem_a, sem_1, sem_2, sem_3, sem_w, sem_f, sem_q1, sem_q2, sem_up, sem_down, sem_h,
 ):
     f32, bf16 = jnp.float32, jnp.bfloat16
     o, i = lax.axis_index("outer"), lax.axis_index("inner")
@@ -110,12 +109,6 @@
     def load(src, dst):
         loads.append(pltpu.make_async_copy(src, dst, sem_in.at[len(loads)]))
         loads[-1].start()
-
-    stores = []
-
-    def store(src, dst):
-        stores.append(pltpu.make_async_copy(src, dst, sem_out.at[len(stores)]))
-        stores[-1].start()
 
     load(cot_in, cot)
     for j in (across, second, first, i):
@@ -271,14 +264,37 @@
     def new_rows(owner):
         return sec_new.at[pl.ds(pl.multiple_of(owner * rows, 128), rows)]
 
-    def store_rows(owner):
-        store(new_rows(owner), sec_out.at[pl.ds(pl.multiple_of(owner * rows, 128), rows)])
-
-    for d in (2, 1, 3):
-        send(new_rows(o), new_rows(o), sem_g, d - 1, (((z + d) % n_z) * 2 + core, i))
+    relayed = []
+
+    def relay(needed, owner, sems, index, peer):
+        copy = pltpu.make_async_remote_copy(
+            src_ref=new_rows(owner), dst_ref=new_rows(owner),
+            send_sem=sems.at[0, index], recv_sem=sems.at[1, index],
+            device_id=(peer, i), device_id_type=MESH,
+        )
+        pl.when(needed)(copy.start)
+        relayed.append((needed, copy))
+
+    def pass_on(t):
+        for way, sems in ((1, sem_up), (-1, sem_down)):
+            owner = o - 2 * t * way
+            here = (z >= t) if way == 1 else (z + t < n_z)
+            if t:
+                pl.when(here)(functools.partial(arrived, new_rows(owner), sems, t - 1))
+            if t < n_z - 1:
+                more = here & ((z < n_z - 1) if way == 1 else (z > 0))
+                relay(more, owner, sems, t, o + 2 * way)
+            if t:
+                relay(here, owner, sem_h, t if way == 1 else 3 + t, mate)
+
+    def from_mate(t):
+        for way in (1, -1):
+            owner = mate - 2 * t * way
+            here = (z >= t) if way == 1 else (z + t < n_z)
+            pl.when(here)(functools.partial(arrived, new_rows(owner), sem_h, t if way == 1 else 3 + t))
+
+    pass_on(0)
     send(new_rows(o), new_rows(o), sem_h, 0, (mate, i))
-    store(master_new, master_out)
-    store_rows(o)
 
     arrived(weights.at[first, core], sem_w, 0)
     send(weights.at[first, core], weights.at[first, core], sem_w, 2, (o, second))
@@ -303,43 +319,30 @@
                 v_row = jnp.maximum(v_row, top)
     m_scale_new[...] = m_row + 1e-06
     v_scale_new[...] = v_row + 1e-06
-    store(m_code_new, m_code_out)
-    store(v_code_new, v_code_out)
-    store(m_scale_new, m_scale_out)
-    store(v_scale_new, v_scale_out)
 
     def product(j, h):
         start = pl.multiple_of(j * span + h * half, 128)
         return jnp.dot(tok[:, pl.ds(start, half)], weights[j, h], preferred_element_type=f32)
 
+    pass_on(1)
     out = out + product(first, core)
     out = out + product(second, core)
-
-    def gathered(d):
-        owner = ((z + n_z - d) % n_z) * 2 + core
-        arrived(new_rows(owner), sem_g, d - 1)
-        send(new_rows(owner), new_rows(owner), sem_h, d, (mate, i))
-        store_rows(owner)
-
-    gathered(1)
-    arrived(weights.at[across, core], sem_w, 2)
-    send(weights.at[across, core], weights.at[across, core], sem_f, 2, (mate, i))
-    out = out + product(across, core)
+    pass_on(2)
     for index, j in enumerate((second, first)):
         arrived(weights.at[j, 1 - core], sem_f, index)
         out = out + product(j, 1 - core)
-    gathered(3)
+    arrived(weights.at[across, core], sem_w, 2)
+    send(weights.at[across, core], weights.at[across, core], sem_f, 2, (mate, i))
+    pass_on(3)
+    out = out + product(across, core)
     arrived(weights.at[across, 1 - core], sem_f, 2)
     out = out + product(across, 1 - core)
     projected[...] = out.astype(bf16)
-    store(projected, projected_out)
-    gathered(2)
-    for d in range(4):
-        owner = ((z + n_z - d) % n_z) * 2 + 1 - core
-        arrived(new_rows(owner), sem_h, d)
-        store_rows(owner)
-    for copy in stores:
-        copy.wait()
+    arrived(new_rows(mate), sem_h, 0)
+    for t in range(1, 4):
+        from_mate(t)
+    for needed, copy in relayed:
+        pl.when(needed)(copy.wait_send)
     for copy in started:
         copy.wait_send()
 
@@ -375,11 +378,10 @@
     work = 4 * tokens.shape[0] * tokens.shape[1] * head
     outs = pl.pallas_call(
         functools.partial(step_kernel, limit),
-        out_shape=[jax.ShapeDtypeStruct(shape, dtype) for shape, dtype in shapes],
+        out_shape=[vmem(shape, dtype) for shape, dtype in shapes],
         in_specs=[pl.BlockSpec(memory_space=pltpu.HBM)] * 8,
-        out_specs=[pl.BlockSpec(memory_space=pltpu.HBM)] * 7,
+        out_specs=[pl.BlockSpec(memory_space=vmem)] * 7,
         scratch_shapes=[
-            *(vmem(shape, dtype) for shape, dtype in shapes),
             vmem(tokens.shape, bf16),
             vmem(cotangent.shape, bf16),
             vmem(secondary.shape, bf16),
@@ -405,7 +407,6 @@
             vmem(chunk, f32),
             vmem(chunk, f32),
             dma((11,)),
-            dma((14,)),
             dma((2, 16)),
             dma((2, 8)),
             dma((2, 4)),
@@ -415,7 +416,8 @@
             dma((2, 3)),
             dma((2, 7)),
             dma((2, 3)),
-            dma((2, 4)),
+            dma((2, 3)),
+            dma((2, 7)),
         ],
         compiler_params=pltpu.CompilerParams(
             collective_id=0, has_side_effects=True, vmem_limit_bytes=VMEM_BYTES
@@ -428,7 +430,7 @@
     outs = pl.pallas_call(
         write_kernel,
         out_shape=[jax.ShapeDtypeStruct(shape, dtype) for shape, dtype in shapes],
-        in_specs=[pl.BlockSpec(memory_space=pltpu.HBM)] * 7,
+        in_specs=[pl.BlockSpec(memory_space=vmem)] * 7,
         out_specs=[pl.BlockSpec(memory_space=pltpu.HBM)] * 7,
         scratch_shapes=[dma((7,))],
         compiler_params=pltpu.CompilerParams(vmem_limit_bytes=VMEM_BYTES),

time: 88.9 us -> 58.4 us (0.66)
  Pallas kernels: 88.1 us -> 53.6 us
  local copies, waits for them, and re-layouts: 0 us -> 3.99 us
    pallas_call x1, Pallas kernels: 37.9 us -> 2.45 us  [fused_body(): pl.pallas_call(write_kernel, out_shape=[jax.ShapeDtypeStruct(shape, dtype...]
    unnamed x0 -> x14, local copies, waits for them, and re-layouts: none -> 3.99 us
    pallas_call x1, Pallas kernels: 50.2 us -> 51.1 us  [fused_body(): pl.pallas_call(functools.partial(step_kernel, limit), out_shape=[vmem(sha...]
where the time goes in v3:
time: 58.4 us; the launch traced here: 58.2 us
  Pallas kernels  53.6 us (92%)
  local copies, waits for them, and re-layouts  3.99 us (7%)
  between operations  0.66 us (1%)
    pallas_call x1, Pallas kernels, fused_body(): pl.pallas_call(functools.partial(step_kernel, limit), out_shape=[vmem(sha...  51.1 us
    unnamed x14, local copies, waits for them, and re-layouts  3.99 us
    pallas_call x1, Pallas kernels, fused_body(): pl.pallas_call(write_kernel, out_shape=[jax.ShapeDtypeStruct(shape, dtype...  2.45 us

profile of v3, /device:TPU:0, one launch (start us, length us, event | category | flops | bytes accessed | tf_op | source)
XLA Modules:
  0.0 58.2 jit_solution(5904696082536215279)
XLA Ops:
  0.6 51.1 %shard_map.135 = (bf16[128,128]{1,0:T(8,128)(2,1)S(1)}, f32[384,128]{1,0:T(8,128)S(1)}, bf16[384,128]{1,0:T(8,128)(2,1)S(1)}, bf16[384,128]{1,0:T(8,128)(2,1)S(1...) custom-call(bf16[128,12288]{1,0:T(8,128)(2,1)} %tok_in.1, bf16[128,128]{1,0:T(8,128)(2,1)} %cot_in.1, ...), custom_call_target="tpu_custom_call" | custom-call | flops 805306368 | bytes 8388608 | tf_op jit(solution)/shard_map/pallas_call | solution.py:379
  51.8 0.0 copy-start
  51.8 0.9 %copy-done = bf16[3072,128]{1,0:T(8,128)(2,1)} copy-done((bf16[3072,128]{1,0:T(8,128)(2,1)}, bf16[3072,128]{1,0:T(8,128)(2,1)S(1)}, u32[]{:S(2)}) %copy-start) | copy-done | bytes 786456
  52.7 0.0 copy-start.1
  52.7 0.7 %copy-done.1 = f32[384,128]{1,0:T(8,128)} copy-done((f32[384,128]{1,0:T(8,128)}, f32[384,128]{1,0:T(8,128)S(1)}, u32[]{:S(2)}) %copy-start.1) | copy-done | bytes 196632
  53.4 0.0 copy-start.2
  53.4 0.6 %copy-done.2 = bf16[384,128]{1,0:T(8,128)(2,1)} copy-done((bf16[384,128]{1,0:T(8,128)(2,1)}, bf16[384,128]{1,0:T(8,128)(2,1)S(1)}, u32[]{:S(2)}) %copy-start.2) | copy-done | bytes 98328
  54.0 0.0 copy-start.3
  54.0 0.6 %copy-done.3 = bf16[384,128]{1,0:T(8,128)(2,1)} copy-done((bf16[384,128]{1,0:T(8,128)(2,1)}, bf16[384,128]{1,0:T(8,128)(2,1)S(1)}, u32[]{:S(2)}) %copy-start.3) | copy-done | bytes 98328
  54.6 0.0 copy-start.4
  54.6 0.6 %copy-done.4 = bf16[128,128]{1,0:T(8,128)(2,1)} copy-done((bf16[128,128]{1,0:T(8,128)(2,1)}, bf16[128,128]{1,0:T(8,128)(2,1)S(1)}, u32[]{:S(2)}) %copy-start.4) | copy-done | bytes 32792
  55.2 0.0 copy-start.5
  55.3 0.0 copy-start.6
  55.3 0.5 copy-done.5
  55.8 0.0 copy-done.6
  55.8 2.5 %shard_map.136 = (bf16[128,128]{1,0:T(8,128)(2,1)}, f32[384,128]{1,0:T(8,128)}, bf16[384,128]{1,0:T(8,128)(2,1)}, bf16[384,128]{1,0:T(8,128)(2,1)}, f32[1,96]{1,...) custom-call(bf16[128,128]{1,0:T(8,128)(2,1)} %copy-done.4, f32[384,128]{1,0:T(8,128)} %copy-done.1, ...), custom_call_target="tpu_custom_call" | custom-call | tf_op jit(solution)/shard_map/pallas_call | solution.py:430
Async XLA Ops:
  51.8 0.9 %copy-start = (bf16[3072,128]{1,0:T(8,128)(2,1)}, bf16[3072,128]{1,0:T(8,128)(2,1)S(1)}, u32[]{:S(2)}) copy-start(bf16[3072,128]{1,0:T(8,128)(2,1)S(1)} %get-tuple-element.27.refs_6_) | copy-start | bytes 2359300
  52.7 0.7 %copy-start.1 = (f32[384,128]{1,0:T(8,128)}, f32[384,128]{1,0:T(8,128)S(1)}, u32[]{:S(2)}) copy-start(f32[384,128]{1,0:T(8,128)S(1)} %get-tuple-element.22.refs_1_) | copy-start | bytes 589828
  53.4 0.6 %copy-start.2 = (bf16[384,128]{1,0:T(8,128)(2,1)}, bf16[384,128]{1,0:T(8,128)(2,1)S(1)}, u32[]{:S(2)}) copy-start(bf16[384,128]{1,0:T(8,128)(2,1)S(1)} %get-tuple-element.23.refs_2_) | copy-start | bytes 294916
  54.0 0.7 %copy-start.3 = (bf16[384,128]{1,0:T(8,128)(2,1)}, bf16[384,128]{1,0:T(8,128)(2,1)S(1)}, u32[]{:S(2)}) copy-start(bf16[384,128]{1,0:T(8,128)(2,1)S(1)} %get-tuple-element.24.refs_3_) | copy-start | bytes 294916
  54.6 0.6 %copy-start.4 = (bf16[128,128]{1,0:T(8,128)(2,1)}, bf16[128,128]{1,0:T(8,128)(2,1)S(1)}, u32[]{:S(2)}) copy-start(bf16[128,128]{1,0:T(8,128)(2,1)S(1)} %get-tuple-element.21.refs_0_) | copy-start | bytes 98308
  55.2 0.5 copy-start.5
  55.3 0.5 copy-start.6

commit v4 on v2

--- a/solution.py
+++ b/solution.py
@@ -78,12 +78,11 @@
 def step_kernel(
     limit,
     tok_in, cot_in, sec_in, master_in, m_code_in, v_code_in, m_scale_in, v_scale_in,
-    projected_out, master_out, m_code_out, v_code_out, m_scale_out, v_scale_out, sec_out,
     projected, master_new, m_code_new, v_code_new, m_scale_new, v_scale_new, sec_new,
     tok, cot, sec, master, m_code, v_code, m_scale, v_scale,
-    send_a, recv_a, send_1, recv_1, sum_2, send_2, recv_2, sum_3, send_3, recv_3,
+    send_a, recv_a, send_1, recv_1, send_2, recv_2, sum_3, send_3, recv_3,
     weights, sq_1, sq_2, sq_send, moments, seconds,
-    sem_in, sem_out, sem_a, sem_1, sem_2, sem_3, sem_w, sem_f, sem_q1, sem_q2, sem_g, sem_h,
+    sem_in, sem_a, sem_1, sem_2, sem_3, sem_w, sem_f, sem_q1, sem_q2, sem_g, sem_h,
 ):
     f32, bf16 = jnp.float32, jnp.bfloat16
     o, i = lax.axis_index("outer"), lax.axis_index("inner")
@@ -111,17 +110,15 @@
         loads.append(pltpu.make_async_copy(src, dst, sem_in.at[len(loads)]))
         loads[-1].start()
 
-    stores = []
-
-    def store(src, dst):
-        stores.append(pltpu.make_async_copy(src, dst, sem_out.at[len(stores)]))
-        stores[-1].start()
-
     load(cot_in, cot)
-    for j in (across, second, first, i):
+    groups = (across, second, first, i)
+    for j in groups[:2]:
         columns = pl.ds(pl.multiple_of(j * span, 128), span)
         load(tok_in.at[:, columns], tok.at[:, columns])
     load(sec_in, sec)
+    for j in groups[2:]:
+        columns = pl.ds(pl.multiple_of(j * span, 128), span)
+        load(tok_in.at[:, columns], tok.at[:, columns])
     load(master_in, master)
     load(m_code_in, m_code)
     load(v_code_in, v_code)
@@ -147,52 +144,68 @@
             device_id=(mate, i), device_id_type=MESH,
         ).wait_recv()
 
-    def partial(j, s, c):
-        block = j * 8 + ((z + STEPS[s]) % n_z) * 2 + c
-        columns = tok[:, pl.ds(pl.multiple_of(block * rows, 128), rows)]
-        return lax.dot_general(
-            columns, cot[...], (((0,), (0,)), ((), ())), preferred_element_type=f32
-        )
-
-    mate_groups = (across, second, first, i)
-    own_groups = (across, first, second, i)
-
-    def for_mate(q):
-        for s in range(4):
-            send_a[q, s] = partial(mate_groups[q], s, 1 - core).astype(bf16)
-            if q == 0 and s == 0:
-                pl.semaphore_wait(barrier, 10)
-            send(send_a.at[q, s], recv_a.at[q, s], sem_a, q * 4 + s, (mate, i))
+    def weight_part(j, part):
+        third = half // 3
+        return weights.at[j, core, pl.ds(part * third, third + part * third)]
+
+    def send_weights(part):
+        third = half // 3
+        start = pl.multiple_of(core * half + part * third, 128)
+        source = sec.at[pl.ds(start, third + part * third)]
+        for index, peer in enumerate((first, second)):
+            send(source, weight_part(i, part), sem_w, 2 * part + index, (o, peer))
+
+    def for_both(g):
+        base = groups[g] * span
+        for k in range(n_z):
+            for c in range(2):
+                start = pl.multiple_of(base + (k * 2 + c) * rows, 128)
+                part = lax.dot_general(
+                    tok[:, pl.ds(start, rows)], cot[...], (((0,), (0,)), ((), ())),
+                    preferred_element_type=f32,
+                )
+                send_a[g, c, k] = part.astype(bf16)
+
+    def to_mate(g):
+        send(send_a.at[g, 1 - core], recv_a.at[g], sem_a, g, (mate, i))
 
     def chip_sum(q, s):
-        own = partial(own_groups[q], s, core)
-        arrived(recv_a.at[q, s], sem_a, q * 4 + s)
-        return own + recv_a[q, s].astype(f32)
+        k = (z + STEPS[s]) % n_z
+        own = send_a[(0, 2, 1, 3)[q], core, k]
+        return own.astype(f32) + recv_a[q, k].astype(f32)
 
     def to_first(q):
+        arrived(recv_a.at[q], sem_a, q)
         for s in range(4):
             send_1[q, s] = chip_sum(q, s).astype(bf16)
             send(send_1.at[q, s], recv_1.at[q, s], sem_1, q * 4 + s, (o, first))
 
     loads[0].wait()
     loads[1].wait()
-    for_mate(0)
+    for_both(0)
+    pl.semaphore_wait(barrier, 10)
+    to_mate(0)
+    loads[3].wait()
+    send_weights(0)
     loads[2].wait()
-    for_mate(1)
+    for_both(1)
+    to_mate(1)
     to_first(0)
-    loads[3].wait()
-    for_mate(2)
+    loads[4].wait()
+    for_both(2)
+    to_mate(2)
     to_first(1)
-    loads[4].wait()
-    for_mate(3)
+    loads[5].wait()
+    for_both(3)
+    to_mate(3)
+    arrived(recv_a.at[2], sem_a, 2)
     for s in range(4):
-        sum_2[s] = chip_sum(2, s)
+        arrived(recv_1.at[0, s], sem_1, s)
+        send_2[s] = (chip_sum(2, s) + recv_1[0, s].astype(f32)).astype(bf16)
+        send(send_2.at[s], recv_2.at[s], sem_2, s, (o, second))
+    arrived(recv_a.at[3], sem_a, 3)
     for s in range(4):
         sum_3[s] = chip_sum(3, s)
-    for s in range(4):
-        arrived(recv_1.at[0, s], sem_1, s)
-        send_2[s] = (sum_2[s] + recv_1[0, s].astype(f32)).astype(bf16)
-        send(send_2.at[s], recv_2.at[s], sem_2, s, (o, second))
 
     for s in range(4):
         arrived(recv_1.at[1, s], sem_1, 4 + s)
@@ -206,10 +219,10 @@
         else:
             sum_3[0] = total
 
-    loads[5].wait()
-    own_half = sec.at[pl.ds(pl.multiple_of(core * half, 128), half)]
-    for index, peer in enumerate((first, second)):
-        send(own_half, weights.at[i, core], sem_w, index, (o, peer))
+    send_weights(1)
+    arrived(weight_part(first, 0), sem_w, 0)
+    send(weight_part(first, 0), weight_part(first, 0), sem_w, 4, (o, second))
+    arrived(weight_part(second, 0), sem_w, 1)
 
     own_columns = tok[:, pl.ds(pl.multiple_of(i * span, 128), span)]
     out = jnp.dot(own_columns, sec[...], preferred_element_type=f32)
@@ -223,15 +236,8 @@
 
     squares = jnp.sum((gradient * gradient).reshape(rows // 8, 8, 128), axis=0)
     sq_send[0] = squares
-    for index, peer in enumerate((first, second, across)):
-        send(sq_send.at[0], sq_1.at[index], sem_q1, index, (o, peer))
-    for index in range(3):
-        arrived(sq_1.at[index], sem_q1, index)
-        squares = squares + sq_1[index]
-    sq_send[1] = squares
     for d in range(1, 8):
-        send(sq_send.at[1], sq_2.at[d - 1], sem_q2, d - 1, ((o + d) % 8, i))
-
+        send(sq_send.at[0], sq_2.at[d - 1], sem_q2, d - 1, ((o + d) % 8, i))
     for copy in loads[6:]:
         copy.wait()
     height = rows // m_scale.shape[1]
@@ -253,6 +259,12 @@
     for d in range(1, 8):
         arrived(sq_2.at[d - 1], sem_q2, d - 1)
         squares = squares + sq_2[d - 1]
+    sq_send[1] = squares
+    for index, peer in enumerate((first, second, across)):
+        send(sq_send.at[1], sq_1.at[index], sem_q1, index, (o, peer))
+    for index in range(3):
+        arrived(sq_1.at[index], sem_q1, index)
+        squares = squares + sq_1[index]
     square_sum = jnp.sum(jnp.sum(squares, axis=0, keepdims=True), axis=1, keepdims=True)
     factor = limit / jnp.maximum(jnp.sqrt(square_sum), limit)
 
@@ -271,19 +283,14 @@
     def new_rows(owner):
         return sec_new.at[pl.ds(pl.multiple_of(owner * rows, 128), rows)]
 
-    def store_rows(owner):
-        store(new_rows(owner), sec_out.at[pl.ds(pl.multiple_of(owner * rows, 128), rows)])
-
     for d in (2, 1, 3):
         send(new_rows(o), new_rows(o), sem_g, d - 1, (((z + d) % n_z) * 2 + core, i))
     send(new_rows(o), new_rows(o), sem_h, 0, (mate, i))
-    store(master_new, master_out)
-    store_rows(o)
-
-    arrived(weights.at[first, core], sem_w, 0)
-    send(weights.at[first, core], weights.at[first, core], sem_w, 2, (o, second))
+
+    arrived(weight_part(first, 1), sem_w, 2)
+    send(weight_part(first, 1), weight_part(first, 1), sem_w, 5, (o, second))
     send(weights.at[first, core], weights.at[first, core], sem_f, 0, (mate, i))
-    arrived(weights.at[second, core], sem_w, 1)
+    arrived(weight_part(second, 1), sem_w, 3)
     send(weights.at[second, core], weights.at[second, core], sem_f, 1, (mate, i))
 
     m_row = jnp.zeros(m_scale.shape, f32)
@@ -303,43 +310,34 @@
                 v_row = jnp.maximum(v_row, top)
     m_scale_new[...] = m_row + 1e-06
     v_scale_new[...] = v_row + 1e-06
-    store(m_code_new, m_code_out)
-    store(v_code_new, v_code_out)
-    store(m_scale_new, m_scale_out)
-    store(v_scale_new, v_scale_out)
 
     def product(j, h):
         start = pl.multiple_of(j * span + h * half, 128)
         return jnp.dot(tok[:, pl.ds(start, half)], weights[j, h], preferred_element_type=f32)
-
-    out = out + product(first, core)
-    out = out + product(second, core)
 
     def gathered(d):
         owner = ((z + n_z - d) % n_z) * 2 + core
         arrived(new_rows(owner), sem_g, d - 1)
         send(new_rows(owner), new_rows(owner), sem_h, d, (mate, i))
-        store_rows(owner)
-
+
+    out = out + product(first, core)
+    out = out + product(second, core)
     gathered(1)
-    arrived(weights.at[across, core], sem_w, 2)
+    arrived(weight_part(across, 0), sem_w, 4)
+    arrived(weight_part(across, 1), sem_w, 5)
     send(weights.at[across, core], weights.at[across, core], sem_f, 2, (mate, i))
     out = out + product(across, core)
+    gathered(3)
     for index, j in enumerate((second, first)):
         arrived(weights.at[j, 1 - core], sem_f, index)
         out = out + product(j, 1 - core)
-    gathered(3)
+    gathered(2)
     arrived(weights.at[across, 1 - core], sem_f, 2)
     out = out + product(across, 1 - core)
     projected[...] = out.astype(bf16)
-    store(projected, projected_out)
-    gathered(2)
     for d in range(4):
         owner = ((z + n_z - d) % n_z) * 2 + 1 - core
         arrived(new_rows(owner), sem_h, d)
-        store_rows(owner)
-    for copy in stores:
-        copy.wait()
     for copy in started:
         copy.wait_send()
 
@@ -375,11 +373,10 @@
     work = 4 * tokens.shape[0] * tokens.shape[1] * head
     outs = pl.pallas_call(
         functools.partial(step_kernel, limit),
-        out_shape=[jax.ShapeDtypeStruct(shape, dtype) for shape, dtype in shapes],
+        out_shape=[vmem(shape, dtype) for shape, dtype in shapes],
         in_specs=[pl.BlockSpec(memory_space=pltpu.HBM)] * 8,
-        out_specs=[pl.BlockSpec(memory_space=pltpu.HBM)] * 7,
+        out_specs=[pl.BlockSpec(memory_space=vmem)] * 7,
         scratch_shapes=[
-            *(vmem(shape, dtype) for shape, dtype in shapes),
             vmem(tokens.shape, bf16),
             vmem(cotangent.shape, bf16),
             vmem(secondary.shape, bf16),
@@ -388,11 +385,10 @@
             vmem(chunk, bf16),
             vmem((1, blocks), f32),
             vmem((1, blocks), f32),
-            vmem((4, 4) + chunk, bf16),
+            vmem((4, 2, 4) + chunk, bf16),
             vmem((4, 4) + chunk, bf16),
             vmem((2, 4) + chunk, bf16),
             vmem((2, 4) + chunk, bf16),
-            vmem((4,) + chunk, f32),
             vmem((4,) + chunk, bf16),
             vmem((4,) + chunk, bf16),
             vmem((4,) + chunk, f32),
@@ -405,12 +401,11 @@
             vmem(chunk, f32),
             vmem(chunk, f32),
             dma((11,)),
-            dma((14,)),
-            dma((2, 16)),
+            dma((2, 4)),
             dma((2, 8)),
             dma((2, 4)),
             dma((2, 3)),
-            dma((2, 3)),
+            dma((2, 6)),
             dma((2, 3)),
             dma((2, 3)),
             dma((2, 7)),
@@ -428,10 +423,10 @@
     outs = pl.pallas_call(
         write_kernel,
         out_shape=[jax.ShapeDtypeStruct(shape, dtype) for shape, dtype in shapes],
-        in_specs=[pl.BlockSpec(memory_space=pltpu.HBM)] * 7,
+        in_specs=[pl.BlockSpec(memory_space=vmem)] * 7,
         out_specs=[pl.BlockSpec(memory_space=pltpu.HBM)] * 7,
         scratch_shapes=[dma((7,))],
-        compiler_params=pltpu.CompilerParams(vmem_limit_bytes=VMEM_BYTES),
+        compiler_params=pltpu.CompilerParams(vmem_limit_bytes=4 << 20),
     )(*outs)
     return (*outs[:4], outs[4].reshape(blocks), outs[5].reshape(blocks), outs[6])
 

time: 88.9 us -> 46.7 us (0.53)
  Pallas kernels: 88.1 us -> 46 us
    pallas_call x1, Pallas kernels: 37.9 us -> 1.09 us  [fused_body(): pl.pallas_call(write_kernel, out_shape=[jax.ShapeDtypeStruct(shape, dtype...]
    pallas_call x1, Pallas kernels: 50.2 us -> 44.9 us  [fused_body(): pl.pallas_call(functools.partial(step_kernel, limit), out_shape=[vmem(sha...]
where the time goes in v4:
time: 46.7 us; the launch traced here: 46.6 us
  Pallas kernels  46 us (99%)
  between operations  0.64 us (1%)
    pallas_call x1, Pallas kernels, fused_body(): pl.pallas_call(functools.partial(step_kernel, limit), out_shape=[vmem(sha...  44.9 us
    pallas_call x1, Pallas kernels, fused_body(): pl.pallas_call(write_kernel, out_shape=[jax.ShapeDtypeStruct(shape, dtype...  1.09 us

profile of v4, /device:TPU:0, one launch (start us, length us, event | category | flops | bytes accessed | tf_op | source)
XLA Modules:
  0.0 46.6 jit_solution(3827630660346672767)
XLA Ops:
  0.6 44.9 %shard_map.135 = (bf16[128,128]{1,0:T(8,128)(2,1)S(1)}, f32[384,128]{1,0:T(8,128)S(1)}, bf16[384,128]{1,0:T(8,128)(2,1)S(1)}, bf16[384,128]{1,0:T(8,128)(2,1)S(1...) custom-call(bf16[128,12288]{1,0:T(8,128)(2,1)} %tok_in.1, bf16[128,128]{1,0:T(8,128)(2,1)} %cot_in.1, ...), custom_call_target="tpu_custom_call" | custom-call | flops 805306368 | bytes 8388608 | tf_op jit(solution)/shard_map/pallas_call | solution.py:374
  45.5 1.1 %shard_map.136 = (bf16[128,128]{1,0:T(8,128)(2,1)}, f32[384,128]{1,0:T(8,128)}, bf16[384,128]{1,0:T(8,128)(2,1)}, bf16[384,128]{1,0:T(8,128)(2,1)}, f32[1,96]{1,...) custom-call(bf16[128,128]{1,0:T(8,128)(2,1)S(1)} %get-tuple-element.21.refs_0_, ...), custom_call_target="tpu_custom_call" | custom-call | tf_op jit(solution)/shard_map/pallas_call | solution.py:423

commit v5 on v4

--- a/solution.py
+++ b/solution.py
@@ -112,13 +112,18 @@
 
     load(cot_in, cot)
     groups = (across, second, first, i)
-    for j in groups[:2]:
-        columns = pl.ds(pl.multiple_of(j * span, 128), span)
-        load(tok_in.at[:, columns], tok.at[:, columns])
-    load(sec_in, sec)
-    for j in groups[2:]:
-        columns = pl.ds(pl.multiple_of(j * span, 128), span)
-        load(tok_in.at[:, columns], tok.at[:, columns])
+    pair = 2 * rows
+
+    def columns_of(g, s):
+        start = groups[g] * span + ((z + STEPS[s]) % n_z) * pair
+        return pl.multiple_of(start, 128)
+
+    for s in range(4):
+        for g in range(4):
+            columns = pl.ds(columns_of(g, s), pair)
+            load(tok_in.at[:, columns], tok.at[:, columns])
+        if s == 0:
+            load(sec_in, sec)
     load(master_in, master)
     load(m_code_in, m_code)
     load(v_code_in, v_code)
@@ -155,69 +160,72 @@
         for index, peer in enumerate((first, second)):
             send(source, weight_part(i, part), sem_w, 2 * part + index, (o, peer))
 
-    def for_both(g):
-        base = groups[g] * span
-        for k in range(n_z):
+    def for_both(s):
+        for g in range(4):
+            loads[1 + 4 * s + g + (s > 0)].wait()
+        for g in range(4):
             for c in range(2):
-                start = pl.multiple_of(base + (k * 2 + c) * rows, 128)
+                start = pl.multiple_of(columns_of(g, s) + c * rows, 128)
                 part = lax.dot_general(
                     tok[:, pl.ds(start, rows)], cot[...], (((0,), (0,)), ((), ())),
                     preferred_element_type=f32,
                 )
-                send_a[g, c, k] = part.astype(bf16)
-
-    def to_mate(g):
-        send(send_a.at[g, 1 - core], recv_a.at[g], sem_a, g, (mate, i))
+                send_a[s, c, g] = part.astype(bf16)
+
+    def to_mate(s):
+        send(send_a.at[s, 1 - core], recv_a.at[s], sem_a, s, (mate, i))
 
     def chip_sum(q, s):
-        k = (z + STEPS[s]) % n_z
-        own = send_a[(0, 2, 1, 3)[q], core, k]
-        return own.astype(f32) + recv_a[q, k].astype(f32)
-
-    def to_first(q):
-        arrived(recv_a.at[q], sem_a, q)
-        for s in range(4):
+        own = send_a[s, core, (0, 2, 1, 3)[q]]
+        return own.astype(f32) + recv_a[s, q].astype(f32)
+
+    def to_first(s):
+        arrived(recv_a.at[s], sem_a, s)
+        for q in range(2):
             send_1[q, s] = chip_sum(q, s).astype(bf16)
             send(send_1.at[q, s], recv_1.at[q, s], sem_1, q * 4 + s, (o, first))
 
-    loads[0].wait()
-    loads[1].wait()
-    for_both(0)
-    pl.semaphore_wait(barrier, 10)
-    to_mate(0)
-    loads[3].wait()
-    send_weights(0)
-    loads[2].wait()
-    for_both(1)
-    to_mate(1)
-    to_first(0)
-    loads[4].wait()
-    for_both(2)
-    to_mate(2)
-    to_first(1)
-    loads[5].wait()
-    for_both(3)
-    to_mate(3)
-    arrived(recv_a.at[2], sem_a, 2)
-    for s in range(4):
+    def to_second(s):
         arrived(recv_1.at[0, s], sem_1, s)
         send_2[s] = (chip_sum(2, s) + recv_1[0, s].astype(f32)).astype(bf16)
         send(send_2.at[s], recv_2.at[s], sem_2, s, (o, second))
-    arrived(recv_a.at[3], sem_a, 3)
-    for s in range(4):
-        sum_3[s] = chip_sum(3, s)
-
-    for s in range(4):
+
+    def along_z(s):
         arrived(recv_1.at[1, s], sem_1, 4 + s)
         arrived(recv_2.at[s], sem_2, s)
-        total = sum_3[s] + recv_1[1, s].astype(f32) + recv_2[s].astype(f32)
+        total = chip_sum(3, s) + recv_1[1, s].astype(f32) + recv_2[s].astype(f32)
         if STEPS[s]:
             d = STEPS[s]
             send_3[d - 1] = total.astype(bf16)
             peer = ((z + d) % n_z) * 2 + core
             send(send_3.at[d - 1], recv_3.at[d - 1], sem_3, d - 1, (peer, i))
         else:
-            sum_3[0] = total
+            sum_3[...] = total
+
+    loads[0].wait()
+    for_both(0)
+    pl.semaphore_wait(barrier, 10)
+    to_mate(0)
+    loads[5].wait()
+    send_weights(0)
+    for_both(1)
+    to_mate(1)
+    to_first(0)
+    for_both(2)
+    to_mate(2)
+    to_first(1)
+    for_both(3)
+    to_mate(3)
+    to_second(0)
+    to_first(2)
+    to_second(1)
+    to_first(3)
+    along_z(0)
+    to_second(2)
+    along_z(1)
+    to_second(3)
+    along_z(2)
+    along_z(3)
 
     send_weights(1)
     arrived(weight_part(first, 0), sem_w, 0)
@@ -229,16 +237,16 @@
 
     for d in (1, 3, 2):
         arrived(recv_3.at[d - 1], sem_3, d - 1)
-    gradient = sum_3[0]
+    gradient = sum_3[...]
     for d in range(1, 4):
         gradient = gradient + recv_3[d - 1].astype(f32)
-    sum_3[0] = gradient
+    sum_3[...] = gradient
 
     squares = jnp.sum((gradient * gradient).reshape(rows // 8, 8, 128), axis=0)
     sq_send[0] = squares
     for d in range(1, 8):
         send(sq_send.at[0], sq_2.at[d - 1], sem_q2, d - 1, ((o + d) % 8, i))
-    for copy in loads[6:]:
+    for copy in loads[18:]:
         copy.wait()
     height = rows // m_scale.shape[1]
 
@@ -270,7 +278,7 @@
 
     for p in range(pieces):
         part = pl.ds(p * PIECE, PIECE)
-        scaled = factor * sum_3[0, part, :]
+        scaled = factor * sum_3[part, :]
         moment = moments[part, :] + 0.1 * scaled
         second_new = seconds[part, :] + 0.05 * scaled * scaled
         old = master[part, :]
@@ -391,7 +399,7 @@
             vmem((2, 4) + chunk, bf16),
             vmem((4,) + chunk, bf16),
             vmem((4,) + chunk, bf16),
-            vmem((4,) + chunk, f32),
+            vmem(chunk, f32),
             vmem((3,) + chunk, bf16),
             vmem((3,) + chunk, bf16),
             vmem((4, 2, secondary.shape[0] // 2, head), bf16),
@@ -400,7 +408,7 @@
             vmem((2, 8, head), f32),
             vmem(chunk, f32),
             vmem(chunk, f32),
-            dma((11,)),
+            dma((23,)),
             dma((2, 4)),
             dma((2, 8)),
             dma((2, 4)),

time: 46.7 us -> 45.7 us (0.979); the launches traced: 46.6 us -> 44.9 us
  Pallas kernels: 46 us -> 44.2 us
    pallas_call x1, Pallas kernels: 44.9 us -> 43.1 us  [fused_body(): pl.pallas_call(functools.partial(step_kernel, limit), out_shape=[vmem(sha...]
where the time goes in v5:
time: 45.7 us; the launch traced here: 44.9 us
  Pallas kernels  44.2 us (97%)
  between operations  0.64 us (1%)
    pallas_call x1, Pallas kernels, fused_body(): pl.pallas_call(functools.partial(step_kernel, limit), out_shape=[vmem(sha...  43.1 us
    pallas_call x1, Pallas kernels, fused_body(): pl.pallas_call(write_kernel, out_shape=[jax.ShapeDtypeStruct(shape, dtype...  1.09 us

profile of v5, /device:TPU:0, one launch (start us, length us, event | category | flops | bytes accessed | tf_op | source)
XLA Modules:
  0.0 44.9 jit_solution(1168197628174022271)
XLA Ops:
  0.6 43.1 %shard_map.135 = (bf16[128,128]{1,0:T(8,128)(2,1)S(1)}, f32[384,128]{1,0:T(8,128)S(1)}, bf16[384,128]{1,0:T(8,128)(2,1)S(1)}, bf16[384,128]{1,0:T(8,128)(2,1)S(1...) custom-call(bf16[128,12288]{1,0:T(8,128)(2,1)} %tok_in.1, bf16[128,128]{1,0:T(8,128)(2,1)} %cot_in.1, ...), custom_call_target="tpu_custom_call" | custom-call | flops 805306368 | bytes 8388608 | tf_op jit(solution)/shard_map/pallas_call | solution.py:382
  43.8 1.1 %shard_map.136 = (bf16[128,128]{1,0:T(8,128)(2,1)}, f32[384,128]{1,0:T(8,128)}, bf16[384,128]{1,0:T(8,128)(2,1)}, bf16[384,128]{1,0:T(8,128)(2,1)}, f32[1,96]{1,...) custom-call(bf16[128,128]{1,0:T(8,128)(2,1)S(1)} %get-tuple-element.21.refs_0_, ...), custom_call_target="tpu_custom_call" | custom-call | tf_op jit(solution)/shard_map/pallas_call | solution.py:431

commit v6 on v5

--- a/solution.py
+++ b/solution.py
@@ -82,7 +82,7 @@
     tok, cot, sec, master, m_code, v_code, m_scale, v_scale,
     send_a, recv_a, send_1, recv_1, send_2, recv_2, sum_3, send_3, recv_3,
     weights, sq_1, sq_2, sq_send, moments, seconds,
-    sem_in, sem_a, sem_1, sem_2, sem_3, sem_w, sem_f, sem_q1, sem_q2, sem_g, sem_h,
+    sem_in, sem_a, sem_1, sem_2, sem_3, sem_w, sem_f, sem_q1, sem_q2, sem_g, sem_h, sem_p, sem_r,
 ):
     f32, bf16 = jnp.float32, jnp.bfloat16
     o, i = lax.axis_index("outer"), lax.axis_index("inner")
@@ -160,20 +160,23 @@
         for index, peer in enumerate((first, second)):
             send(source, weight_part(i, part), sem_w, 2 * part + index, (o, peer))
 
+    def partials(s, c):
+        for g in range(4):
+            start = pl.multiple_of(columns_of(g, s) + c * rows, 128)
+            part = lax.dot_general(
+                tok[:, pl.ds(start, rows)], cot[...], (((0,), (0,)), ((), ())),
+                preferred_element_type=f32,
+            )
+            send_a[s, c, g] = part.astype(bf16)
+
     def for_both(s):
         for g in range(4):
             loads[1 + 4 * s + g + (s > 0)].wait()
-        for g in range(4):
-            for c in range(2):
-                start = pl.multiple_of(columns_of(g, s) + c * rows, 128)
-                part = lax.dot_general(
-                    tok[:, pl.ds(start, rows)], cot[...], (((0,), (0,)), ((), ())),
-                    preferred_element_type=f32,
-                )
-                send_a[s, c, g] = part.astype(bf16)
-
-    def to_mate(s):
+        partials(s, 1 - core)
+        if s == 0:
+            pl.semaphore_wait(barrier, 10)
         send(send_a.at[s, 1 - core], recv_a.at[s], sem_a, s, (mate, i))
+        partials(s, core)
 
     def chip_sum(q, s):
         own = send_a[s, core, (0, 2, 1, 3)[q]]
@@ -204,18 +207,13 @@
 
     loads[0].wait()
     for_both(0)
-    pl.semaphore_wait(barrier, 10)
-    to_mate(0)
     loads[5].wait()
     send_weights(0)
     for_both(1)
-    to_mate(1)
     to_first(0)
     for_both(2)
-    to_mate(2)
     to_first(1)
     for_both(3)
-    to_mate(3)
     to_second(0)
     to_first(2)
     to_second(1)
@@ -276,6 +274,12 @@
     square_sum = jnp.sum(jnp.sum(squares, axis=0, keepdims=True), axis=1, keepdims=True)
     factor = limit / jnp.maximum(jnp.sqrt(square_sum), limit)
 
+    def new_rows(owner):
+        return sec_new.at[pl.ds(pl.multiple_of(owner * rows, 128), rows)]
+
+    def new_piece(owner, p):
+        return sec_new.at[pl.ds(pl.multiple_of(owner * rows + p * PIECE, 128), PIECE)]
+
     for p in range(pieces):
         part = pl.ds(p * PIECE, PIECE)
         scaled = factor * sum_3[part, :]
@@ -287,12 +291,19 @@
         seconds[part, :] = second_new
         master_new[part, :] = new
         sec_new[pl.ds(pl.multiple_of(o * rows + p * PIECE, 128), PIECE), :] = new.astype(bf16)
-
-    def new_rows(owner):
-        return sec_new.at[pl.ds(pl.multiple_of(owner * rows, 128), rows)]
-
-    for d in (2, 1, 3):
-        send(new_rows(o), new_rows(o), sem_g, d - 1, (((z + d) % n_z) * 2 + core, i))
+        send(new_piece(o, p), new_piece(o, p), sem_p, p, (((z + 2) % n_z) * 2 + core, i))
+
+    def neighbour(d):
+        peer = (((z + d) % n_z) * 2 + core, i)
+        return pltpu.make_async_remote_copy(
+            src_ref=new_rows(o), dst_ref=new_rows(o),
+            send_sem=sem_g.at[0, d - 1], recv_sem=sem_g.at[1, d - 1],
+            device_id=peer, device_id_type=MESH,
+        )
+
+    guarded = [(z < n_z - 1, neighbour(1)), (z > 0, neighbour(3))]
+    for needed, copy in guarded:
+        pl.when(needed)(copy.start)
     send(new_rows(o), new_rows(o), sem_h, 0, (mate, i))
 
     arrived(weight_part(first, 1), sem_w, 2)
@@ -325,21 +336,35 @@
 
     def gathered(d):
         owner = ((z + n_z - d) % n_z) * 2 + core
-        arrived(new_rows(owner), sem_g, d - 1)
+        if d != 2:
+            arrived(new_rows(owner), sem_g, d - 1)
+        else:
+            for p in range(pieces):
+                arrived(new_piece(owner, p), sem_p, p)
+            inside = (z > 0) & (z < n_z - 1)
+            index = (2 * z + 2) % n_z
+            end = (z // 2) * (n_z - 1)
+            copy = pltpu.make_async_remote_copy(
+                src_ref=new_rows(owner), dst_ref=new_rows(owner),
+                send_sem=sem_r.at[0], recv_sem=sem_g.at[1, index],
+                device_id=(end * 2 + core, i), device_id_type=MESH,
+            )
+            pl.when(inside)(copy.start)
+            guarded.append((inside, copy))
         send(new_rows(owner), new_rows(owner), sem_h, d, (mate, i))
 
     out = out + product(first, core)
     out = out + product(second, core)
-    gathered(1)
+    gathered(2)
     arrived(weight_part(across, 0), sem_w, 4)
     arrived(weight_part(across, 1), sem_w, 5)
     send(weights.at[across, core], weights.at[across, core], sem_f, 2, (mate, i))
     out = out + product(across, core)
-    gathered(3)
     for index, j in enumerate((second, first)):
         arrived(weights.at[j, 1 - core], sem_f, index)
         out = out + product(j, 1 - core)
-    gathered(2)
+    gathered(1)
+    gathered(3)
     arrived(weights.at[across, 1 - core], sem_f, 2)
     out = out + product(across, 1 - core)
     projected[...] = out.astype(bf16)
@@ -348,6 +373,8 @@
         arrived(new_rows(owner), sem_h, d)
     for copy in started:
         copy.wait_send()
+    for needed, copy in guarded:
+        pl.when(needed)(copy.wait_send)
 
 
 def write_kernel(*refs):
@@ -419,6 +446,8 @@
             dma((2, 7)),
             dma((2, 3)),
             dma((2, 4)),
+            dma((2, 3)),
+            dma((1,)),
         ],
         compiler_params=pltpu.CompilerParams(
             collective_id=0, has_side_effects=True, vmem_limit_bytes=VMEM_BYTES

time: 45.7 us -> 45.4 us (level); the launches traced: 44.9 us -> 45.2 us
  no operation moved by 1% of the time
where the time goes in v6:
time: 45.4 us; the launch traced here: 45.2 us
  Pallas kernels  44.6 us (98%)
  between operations  0.64 us (1%)
    pallas_call x1, Pallas kernels, fused_body(): pl.pallas_call(functools.partial(step_kernel, limit), out_shape=[vmem(sha...  43.5 us
    pallas_call x1, Pallas kernels, fused_body(): pl.pallas_call(write_kernel, out_shape=[jax.ShapeDtypeStruct(shape, dtype...  1.09 us

profile of v6, /device:TPU:0, one launch (start us, length us, event | category | flops | bytes accessed | tf_op | source)
XLA Modules:
  0.0 45.2 jit_solution(13154104660621531814)
XLA Ops:
  0.6 43.5 %shard_map.135 = (bf16[128,128]{1,0:T(8,128)(2,1)S(1)}, f32[384,128]{1,0:T(8,128)S(1)}, bf16[384,128]{1,0:T(8,128)(2,1)S(1)}, bf16[384,128]{1,0:T(8,128)(2,1)S(1...) custom-call(bf16[128,12288]{1,0:T(8,128)(2,1)} %tok_in.1, bf16[128,128]{1,0:T(8,128)(2,1)} %cot_in.1, ...), custom_call_target="tpu_custom_call" | custom-call | flops 805306368 | bytes 8388608 | tf_op jit(solution)/shard_map/pallas_call | solution.py:409
  44.1 1.1 %shard_map.136 = (bf16[128,128]{1,0:T(8,128)(2,1)}, f32[384,128]{1,0:T(8,128)}, bf16[384,128]{1,0:T(8,128)(2,1)}, bf16[384,128]{1,0:T(8,128)(2,1)}, f32[1,96]{1,...) custom-call(bf16[128,128]{1,0:T(8,128)(2,1)S(1)} %get-tuple-element.21.refs_0_, ...), custom_call_target="tpu_custom_call" | custom-call | tf_op jit(solution)/shard_map/pallas_call | solution.py:460

commit v7 on v6

--- a/solution.py
+++ b/solution.py
@@ -268,6 +268,12 @@
     sq_send[1] = squares
     for index, peer in enumerate((first, second, across)):
         send(sq_send.at[1], sq_1.at[index], sem_q1, index, (o, peer))
+    arrived(weight_part(first, 1), sem_w, 2)
+    send(weight_part(first, 1), weight_part(first, 1), sem_w, 5, (o, second))
+    send(weights.at[first, core], weights.at[first, core], sem_f, 0, (mate, i))
+    arrived(weight_part(second, 1), sem_w, 3)
+    send(weights.at[second, core], weights.at[second, core], sem_f, 1, (mate, i))
+
     for index in range(3):
         arrived(sq_1.at[index], sem_q1, index)
         squares = squares + sq_1[index]
@@ -305,12 +311,6 @@
     for needed, copy in guarded:
         pl.when(needed)(copy.start)
     send(new_rows(o), new_rows(o), sem_h, 0, (mate, i))
-
-    arrived(weight_part(first, 1), sem_w, 2)
-    send(weight_part(first, 1), weight_part(first, 1), sem_w, 5, (o, second))
-    send(weights.at[first, core], weights.at[first, core], sem_f, 0, (mate, i))
-    arrived(weight_part(second, 1), sem_w, 3)
-    send(weights.at[second, core], weights.at[second, core], sem_f, 1, (mate, i))
 
     m_row = jnp.zeros(m_scale.shape, f32)
     v_row = jnp.zeros(v_scale.shape, f32)

time: 45.4 us -> 45.4 us (level)
  no operation moved by 1% of the time
where the time goes in v7:
time: 45.4 us; the launch traced here: 45.2 us
  Pallas kernels  44.6 us (98%)
  between operations  0.64 us (1%)
    pallas_call x1, Pallas kernels, fused_body(): pl.pallas_call(functools.partial(step_kernel, limit), out_shape=[vmem(sha...  43.5 us
    pallas_call x1, Pallas kernels, fused_body(): pl.pallas_call(write_kernel, out_shape=[jax.ShapeDtypeStruct(shape, dtype...  1.09 us

profile of v7, /device:TPU:0, one launch (start us, length us, event | category | flops | bytes accessed | tf_op | source)
XLA Modules:
  0.0 45.2 jit_solution(7125876440798645028)
XLA Ops:
  0.6 43.5 %shard_map.135 = (bf16[128,128]{1,0:T(8,128)(2,1)S(1)}, f32[384,128]{1,0:T(8,128)S(1)}, bf16[384,128]{1,0:T(8,128)(2,1)S(1)}, bf16[384,128]{1,0:T(8,128)(2,1)S(1...) custom-call(bf16[128,12288]{1,0:T(8,128)(2,1)} %tok_in.1, bf16[128,128]{1,0:T(8,128)(2,1)} %cot_in.1, ...), custom_call_target="tpu_custom_call" | custom-call | flops 805306368 | bytes 8388608 | tf_op jit(solution)/shard_map/pallas_call | solution.py:409
  44.1 1.1 %shard_map.136 = (bf16[128,128]{1,0:T(8,128)(2,1)}, f32[384,128]{1,0:T(8,128)}, bf16[384,128]{1,0:T(8,128)(2,1)}, bf16[384,128]{1,0:T(8,128)(2,1)}, f32[1,96]{1,...) custom-call(bf16[128,128]{1,0:T(8,128)(2,1)S(1)} %get-tuple-element.21.refs_0_, ...), custom_call_target="tpu_custom_call" | custom-call | tf_op jit(solution)/shard_map/pallas_call | solution.py:460

commit v8 on v7

--- a/solution.py
+++ b/solution.py
@@ -207,8 +207,6 @@
 
     loads[0].wait()
     for_both(0)
-    loads[5].wait()
-    send_weights(0)
     for_both(1)
     to_first(0)
     for_both(2)
@@ -225,6 +223,8 @@
     along_z(2)
     along_z(3)
 
+    loads[5].wait()
+    send_weights(0)
     send_weights(1)
     arrived(weight_part(first, 0), sem_w, 0)
     send(weight_part(first, 0), weight_part(first, 0), sem_w, 4, (o, second))

time: 45.4 us -> 48.8 us (1.075)
  Pallas kernels: 44.6 us -> 48 us
    pallas_call x1, Pallas kernels: 43.5 us -> 46.9 us  [fused_body(): pl.pallas_call(functools.partial(step_kernel, limit), out_shape=[vmem(sha...]
where the time goes in v8:
time: 48.8 us; the launch traced here: 48.6 us
  Pallas kernels  48 us (98%)
  between operations  0.64 us (1%)
    pallas_call x1, Pallas kernels, fused_body(): pl.pallas_call(functools.partial(step_kernel, limit), out_shape=[vmem(sha...  46.9 us
    pallas_call x1, Pallas kernels, fused_body(): pl.pallas_call(write_kernel, out_shape=[jax.ShapeDtypeStruct(shape, dtype...  1.09 us

profile of v8, /device:TPU:0, one launch (start us, length us, event | category | flops | bytes accessed | tf_op | source)
XLA Modules:
  0.0 48.6 jit_solution(9165511907306235231)
XLA Ops:
  0.6 46.9 %shard_map.135 = (bf16[128,128]{1,0:T(8,128)(2,1)S(1)}, f32[384,128]{1,0:T(8,128)S(1)}, bf16[384,128]{1,0:T(8,128)(2,1)S(1)}, bf16[384,128]{1,0:T(8,128)(2,1)S(1...) custom-call(bf16[128,12288]{1,0:T(8,128)(2,1)} %tok_in.1, bf16[128,128]{1,0:T(8,128)(2,1)} %cot_in.1, ...), custom_call_target="tpu_custom_call" | custom-call | flops 805306368 | bytes 8388608 | tf_op jit(solution)/shard_map/pallas_call | solution.py:409
  47.6 1.1 %shard_map.136 = (bf16[128,128]{1,0:T(8,128)(2,1)}, f32[384,128]{1,0:T(8,128)}, bf16[384,128]{1,0:T(8,128)(2,1)}, bf16[384,128]{1,0:T(8,128)(2,1)}, f32[1,96]{1,...) custom-call(bf16[128,128]{1,0:T(8,128)(2,1)S(1)} %get-tuple-element.21.refs_0_, ...), custom_call_target="tpu_custom_call" | custom-call | tf_op jit(solution)/shard_map/pallas_call | solution.py:460

commit v9 on v7

--- a/solution.py
+++ b/solution.py
@@ -151,12 +151,12 @@
 
     def weight_part(j, part):
         third = half // 3
-        return weights.at[j, core, pl.ds(part * third, third + part * third)]
+        return weights.at[j, core, pl.ds(2 * part * third, (2 - part) * third)]
 
     def send_weights(part):
         third = half // 3
-        start = pl.multiple_of(core * half + part * third, 128)
-        source = sec.at[pl.ds(start, third + part * third)]
+        start = pl.multiple_of(core * half + 2 * part * third, 128)
+        source = sec.at[pl.ds(start, (2 - part) * third)]
         for index, peer in enumerate((first, second)):
             send(source, weight_part(i, part), sem_w, 2 * part + index, (o, peer))
 

time: 45.4 us -> 48 us (1.057)
  Pallas kernels: 44.6 us -> 47.2 us
    pallas_call x1, Pallas kernels: 43.5 us -> 46.2 us  [fused_body(): pl.pallas_call(functools.partial(step_kernel, limit), out_shape=[vmem(sha...]
where the time goes in v9:
time: 48 us; the launch traced here: 47.9 us
  Pallas kernels  47.2 us (98%)
  between operations  0.64 us (1%)
    pallas_call x1, Pallas kernels, fused_body(): pl.pallas_call(functools.partial(step_kernel, limit), out_shape=[vmem(sha...  46.2 us
    pallas_call x1, Pallas kernels, fused_body(): pl.pallas_call(write_kernel, out_shape=[jax.ShapeDtypeStruct(shape, dtype...  1.09 us

profile of v9, /device:TPU:0, one launch (start us, length us, event | category | flops | bytes accessed | tf_op | source)
XLA Modules:
  0.0 47.9 jit_solution(13745553706726311053)
XLA Ops:
  0.6 46.2 %shard_map.135 = (bf16[128,128]{1,0:T(8,128)(2,1)S(1)}, f32[384,128]{1,0:T(8,128)S(1)}, bf16[384,128]{1,0:T(8,128)(2,1)S(1)}, bf16[384,128]{1,0:T(8,128)(2,1)S(1...) custom-call(bf16[128,12288]{1,0:T(8,128)(2,1)} %tok_in.1, bf16[128,128]{1,0:T(8,128)(2,1)} %cot_in.1, ...), custom_call_target="tpu_custom_call" | custom-call | flops 805306368 | bytes 8388608 | tf_op jit(solution)/shard_map/pallas_call | solution.py:409
  46.8 1.1 %shard_map.136 = (bf16[128,128]{1,0:T(8,128)(2,1)}, f32[384,128]{1,0:T(8,128)}, bf16[384,128]{1,0:T(8,128)(2,1)}, bf16[384,128]{1,0:T(8,128)(2,1)}, f32[1,96]{1,...) custom-call(bf16[128,128]{1,0:T(8,128)(2,1)S(1)} %get-tuple-element.21.refs_0_, ...), custom_call_target="tpu_custom_call" | custom-call | tf_op jit(solution)/shard_map/pallas_call | solution.py:460
